TPU v7x, 512 devices: a whole 4x4x16 slice. The times are simulated.
512 devices in a mesh: dp: 64 (over z, x_hi, core), tensor: 8 (over x_lo, y).
Axes of the slice: x: 4 (x_hi: 2, x_lo: 2; x = x_hi * 2 + x_lo), y: 4, z: 16, core: 2. Of those that a mesh axis runs over, the one named last changes fastest.
Arguments:
- gate_values: bfloat16 [8192, 14336], P('dp', 'tensor'), may hold values from -6 to 6
- up_values: bfloat16 [8192, 14336], P('dp', 'tensor'), may hold values from -6 to 6
- output_grad: bfloat16 [8192, 4096], P(('dp', 'tensor')), may hold values from -6 to 6
- kept_columns: int32 [224, 16], P('tensor'), may hold values from 0 to 63, as said below
- block_owner: int32 [224, 16], P('tensor'), may hold values from 0 to 63, as said below
- master_blocks: float32 [64, 8, 8, 4096], P('dp', 'tensor'), may hold values from -0.09375 to 0.09375
Outputs:
- layer_output: bfloat16 [8192, 4096], P(('dp', 'tensor'))
- gate_grad: bfloat16 [8192, 14336], P('dp', 'tensor')
- up_grad: bfloat16 [8192, 14336], P('dp', 'tensor')
- master_grads: float32 [64, 8, 8, 4096], P('dp', 'tensor')
Inputs may be any that keep to these rules, and one draw needn't show every extreme that they name: `kept_columns`: row r lists the 16 different column blocks kept in block row r, in increasing order. `block_owner`: within one part (28 block rows), no dp index owns more than 8 blocks, and some dp index owns exactly 8.
All inputs are finite; a program needn't handle non-finite values.
Results may differ from a plain program's by a relative error of at most 0.017.
Values may be sent and summed in bfloat16 or wider, within the bound.
No kernel may reach another device: no remote copies, remote signals or barrier semaphores. Data moves between devices by JAX's collectives and lax.ppermute only.
A program may use at most 128 MiB of HBM per device.

v0:
```python
import jax
import jax.numpy as jnp
from jax import lax
from jax.sharding import PartitionSpec as P

BLOCK = 64


def slot_ranks(owner_list, owner_count):
    flat_owner = owner_list.reshape(-1)
    owner_ids = jnp.arange(owner_count, dtype=jnp.int32)
    membership = (flat_owner[:, None] == owner_ids[None, :]).astype(jnp.int32)
    earlier = jnp.cumsum(membership, axis=0) - membership
    return jnp.sum(earlier * membership, axis=1)


def on_device(gate_values, up_values, output_grad, kept_columns, block_owner, master_blocks):
    block_size = BLOCK
    row_count = gate_values.shape[0]
    model_width = output_grad.shape[1]
    col_blocks = model_width // block_size
    row_blocks, kept_count = kept_columns.shape
    capacity = master_blocks.shape[2]
    owner_count = lax.axis_size("dp")
    square = block_size * block_size
    gate_wide = gate_values.astype(jnp.float32)
    up_wide = up_values.astype(jnp.float32)
    sigmoid_gate = jax.nn.sigmoid(gate_wide)
    swish_gate = gate_wide * sigmoid_gate
    hidden = (swish_gate * up_wide).astype(jnp.bfloat16)
    full_grad = lax.all_gather(output_grad, "tensor", axis=0, tiled=True)
    stored = master_blocks.reshape(capacity, square).astype(jnp.bfloat16)
    arrived = lax.all_gather(stored, "dp", axis=0, tiled=True)
    slot_rank = slot_ranks(block_owner, owner_count)
    positions = block_owner.reshape(-1) * capacity + slot_rank
    position_grid = positions.reshape(row_blocks, kept_count)
    hidden_blocks = hidden.reshape(row_count, row_blocks, block_size)
    grad_blocks = full_grad.reshape(row_count, col_blocks, block_size)
    row_group = max((divisor for divisor in range(1, 9) if row_blocks % divisor == 0))
    turn_count = row_blocks // row_group

    def step(out_acc, turn_index):
        first_row = turn_index * row_group
        part_hidden = lax.dynamic_slice_in_dim(hidden_blocks, first_row, row_group, 1)
        part_pos = lax.dynamic_slice_in_dim(position_grid, first_row, row_group, 0).reshape(-1)
        part_weights = jnp.take(arrived, part_pos, axis=0).reshape(
            row_group, kept_count, block_size, block_size
        )
        part_cols = lax.dynamic_slice_in_dim(kept_columns, first_row, row_group, 0).reshape(-1)
        chosen = jnp.take(grad_blocks, part_cols, axis=1).reshape(
            row_count, row_group, kept_count, block_size
        )
        forward = jnp.einsum(
            "tgi,gkij->tgkj", part_hidden, part_weights, preferred_element_type=jnp.float32
        )
        out_acc = out_acc.at[:, part_cols].add(
            forward.reshape(row_count, row_group * kept_count, block_size)
        )
        backward = jnp.einsum(
            "tgkj,gkij->tgi", chosen, part_weights, preferred_element_type=jnp.float32
        )
        local = jnp.einsum(
            "tgi,tgkj->gkij", part_hidden, chosen, preferred_element_type=jnp.float32
        )
        return (out_acc, (backward, local))

    start_acc = jnp.zeros((row_count, col_blocks, block_size), jnp.float32)
    out_acc, (back_stack, local_stack) = lax.scan(
        step, start_acc, jnp.arange(turn_count, dtype=jnp.int32)
    )
    partial_out = out_acc.reshape(row_count, model_width)
    layer_output = lax.psum_scatter(
        partial_out.astype(jnp.bfloat16), "tensor", scatter_dimension=0, tiled=True
    )
    hidden_grad = jnp.transpose(back_stack, (1, 0, 2, 3)).reshape(
        row_count, row_blocks * block_size
    )
    up_grad = (hidden_grad * swish_gate).astype(jnp.bfloat16)
    gate_grad = (
        hidden_grad * up_wide * sigmoid_gate * (1.0 + gate_wide * (1.0 - sigmoid_gate))
    ).astype(jnp.bfloat16)
    send_grads = jnp.zeros((owner_count * capacity, square), jnp.float32)
    send_grads = send_grads.at[positions].set(local_stack.reshape(-1, square))
    owner_grads = send_grads.reshape(owner_count, capacity, square)
    arrived_grads = lax.all_to_all(owner_grads, "dp", split_axis=0, concat_axis=0, tiled=True)
    summed_grads = jnp.sum(arrived_grads, axis=0)
    scale_factor = float(row_count * owner_count) ** (-0.5)
    master_grads = (summed_grads * scale_factor).reshape(1, 1, capacity, square)
    return (layer_output, gate_grad, up_grad, master_grads)


def solution(mesh):
    return jax.shard_map(
        on_device,
        mesh=mesh,
        in_specs=(
            P("dp", "tensor"),
            P("dp", "tensor"),
            P(("dp", "tensor"), None),
            P("tensor", None),
            P("tensor", None),
            P("dp", "tensor", None, None),
        ),
        out_specs=(
            P(("dp", "tensor"), None),
            P("dp", "tensor"),
            P("dp", "tensor"),
            P("dp", "tensor", None, None),
        ),
        check_vma=False,
    )
```

profile of v0, /device:TPU:6, one launch (start us, length us, event | category | flops | bytes accessed | tf_op | source)
XLA Modules:
  0.0 813.4 jit_solution(140619716787221674)
XLA Ops:
  16.8 43.7 %all-gather.4.cloned.1.call-done = bf16[128,4096]{1,0:T(8,128)(2,1)} async-done(((bf16[16,4096]{1,0:T(8,128)(2,1)}), bf16[128,4096]{1,0:T(8,128)(2,1)}) %all-gather.4.cloned.1.call-update) | async-done | bytes 1048592 | tf_op jit(solution)/shard_map/all_gather | solution.py:31
  62.1 151.5 %all-gather.6.cloned.1.call-done = bf16[1,1,512,4096]{3,2,1,0:T(8,128)(2,1)} async-done(((bf16[1,1,8,4096]{3,2,1,0:T(8,128)(2,1)}), bf16[1,1,512,4096]{3,2,1,0:T(8,128)(2,1)}) %all-gather.6.cloned.1.call-update) | async-done | bytes 4194320 | tf_op jit(solution)/shard_map/all_gather | solution.py:33
  213.9 183.0 %while.14 = (s32[]{:T(128)}, f32[128,64,64]{0,2,1:T(8,128)S(1)}, f32[4,128,7,64]{1,3,2,0:T(8,128)}, f32[4,7,16,64,64]{4,3,2,1,0:T(8,128)}, s32[4]{0:T(128)S(1)},...) while((s32[]{:T(128)}, f32[128,64,64]{0,2,1:T(8,128)S(1)}, ...), condition=%wide.region_5.6_spmd, body=%wide.region_3.5_spmd.sunk | while | flops 355995616 | bytes 45433172 | solution.py:68
  215.4 5.7 gather_fusion
  221.1 3.8 gather.21
  234.4 11.8 %scatter_fusion = f32[128,64,64]{0,2,1:T(8,128)S(1)} fusion(f32[128,64,64]{0,2,1:T(8,128)S(1)} %get-tuple-element.227, s32[112]{0:T(128)S(1)} %fusion.41, f32[112,128,64]{1,2,0:T(8,128)} %bitcast.83), kind=kCustom, calls=%fused_computation.2.clone.1 | custom fusion | flops 917504 | bytes 11010496 | tf_op jit(solution)/shard_map/while/body/eval_jaxpr/scatter-add | solution.py:56
  246.2 4.1 convolution_bitcast_fusion.2
  250.3 5.0 copy.69
  255.3 4.3 constant_dynamic-update-slice_fusion.2
  261.1 5.7 gather_fusion
  266.8 3.8 gather.21
  280.1 11.8 %scatter_fusion = f32[128,64,64]{0,2,1:T(8,128)S(1)} fusion(f32[128,64,64]{0,2,1:T(8,128)S(1)} %get-tuple-element.227, s32[112]{0:T(128)S(1)} %fusion.41, f32[112,128,64]{1,2,0:T(8,128)} %bitcast.83), kind=kCustom, calls=%fused_computation.2.clone.1 | custom fusion | flops 917504 | bytes 11010496 | tf_op jit(solution)/shard_map/while/body/eval_jaxpr/scatter-add | solution.py:56
  291.9 4.1 convolution_bitcast_fusion.2
  296.0 5.0 copy.69
  301.0 4.4 constant_dynamic-update-slice_fusion.2
  306.9 5.7 gather_fusion
  312.5 3.8 gather.21
  325.8 11.8 %scatter_fusion = f32[128,64,64]{0,2,1:T(8,128)S(1)} fusion(f32[128,64,64]{0,2,1:T(8,128)S(1)} %get-tuple-element.227, s32[112]{0:T(128)S(1)} %fusion.41, f32[112,128,64]{1,2,0:T(8,128)} %bitcast.83), kind=kCustom, calls=%fused_computation.2.clone.1 | custom fusion | flops 917504 | bytes 11010496 | tf_op jit(solution)/shard_map/while/body/eval_jaxpr/scatter-add | solution.py:56
  337.7 4.1 convolution_bitcast_fusion.2
  341.8 5.0 copy.69
  346.8 4.3 constant_dynamic-update-slice_fusion.2
  352.6 5.7 gather_fusion
  358.3 3.8 gather.21
  371.6 11.8 %scatter_fusion = f32[128,64,64]{0,2,1:T(8,128)S(1)} fusion(f32[128,64,64]{0,2,1:T(8,128)S(1)} %get-tuple-element.227, s32[112]{0:T(128)S(1)} %fusion.41, f32[112,128,64]{1,2,0:T(8,128)} %bitcast.83), kind=kCustom, calls=%fused_computation.2.clone.1 | custom fusion | flops 917504 | bytes 11010496 | tf_op jit(solution)/shard_map/while/body/eval_jaxpr/scatter-add | solution.py:56
  383.4 4.1 convolution_bitcast_fusion.2
  387.5 5.0 copy.69
  392.5 4.4 constant_dynamic-update-slice_fusion.2
  396.9 12.9 %reshape.204 = f32[448,4096]{1,0:T(8,128)} reshape(f32[4,7,16,64,64]{4,3,2,1,0:T(8,128)} %get-tuple-element.60) | data formatting | bytes 14680064 | tf_op jit(solution)/shard_map/reshape | solution.py:83
  409.8 11.2 %scatter_custom_fusion.1 = f32[512,4096]{1,0:T(8,128)} fusion(s32[448]{0:T(512)S(1)} %bitcast.92, f32[448,4096]{1,0:T(8,128)} %reshape.204, f32[]{:T(128)} %constant.43.clone.1), kind=kCustom, calls=%fused_computation.37 | custom fusion | bytes 8389120 | tf_op jit(solution)/shard_map/scatter | solution.py:83
  421.0 10.8 %all-to-all-start = ((f32[64,8,4096]{2,1,0:T(8,128)}), f32[64,8,4096]{2,1,0:T(8,128)}, u32[]{:S(2)}, u32[]{:S(2)}) async-start(f32[64,8,4096]{2,1,0:T(8,128)} %bitcast.88), calls=%async_computation | async-start | bytes 16777216 | tf_op jit(solution)/shard_map/all_to_all | solution.py:85
  437.3 365.1 %all-to-all-done = f32[64,8,4096]{2,1,0:T(8,128)} async-done(((f32[64,8,4096]{2,1,0:T(8,128)}), f32[64,8,4096]{2,1,0:T(8,128)}, u32[]{:S(2)}, u32[]{:S(2)}) %all-to-all-start) | async-done | bytes 8388640 | tf_op jit(solution)/shard_map/all_to_all | solution.py:85
  802.4 3.8 reduce_sum.25
  (93 shorter events, 58.7 us)
Async XLA Ops:
  7.2 53.3 %all-gather.4.cloned.1.call-start = ((), (), s32[]{:S(2)}) async-start(), calls=%async_computation.2 | async-start | bytes 1179648 | tf_op jit(solution)/shard_map/all_gather | solution.py:31
  7.9 205.8 %all-gather.6.cloned.1.call-start = ((), (), s32[]{:S(2)}) async-start(), calls=%async_computation.3 | async-start | bytes 4259840 | tf_op jit(solution)/shard_map/all_gather | solution.py:33
  14.3 199.3 %copy-start.1 = (bf16[128,1792]{0,1:T(8,128)(2,1)}, bf16[128,1792]{0,1:T(8,128)(2,1)S(1)}, u32[]{:S(2)}) copy-start(bf16[128,1792]{0,1:T(8,128)(2,1)S(1)} %copy.48) | copy-start | bytes 1376260
  15.8 197.9 %copy-start.2 = (bf16[128,1792]{0,1:T(8,128)(2,1)}, bf16[128,1792]{0,1:T(8,128)(2,1)S(1)}, u32[]{:S(2)}) copy-start(bf16[128,1792]{0,1:T(8,128)(2,1)S(1)} %copy.49) | copy-start | bytes 1376260
  226.9 3.7 copy-start
  272.7 3.7 copy-start
  318.4 3.7 copy-start
  364.1 3.7 copy-start
  421.0 381.4 %all-to-all-start = ((f32[64,8,4096]{2,1,0:T(8,128)}), f32[64,8,4096]{2,1,0:T(8,128)}, u32[]{:S(2)}, u32[]{:S(2)}) async-start(f32[64,8,4096]{2,1,0:T(8,128)} %bitcast.88), calls=%async_computation | async-start | bytes 16777216 | tf_op jit(solution)/shard_map/all_to_all | solution.py:85
  431.8 375.0 %reduce-scatter.4.cloned.1.call-start = ((), (), s32[]{:S(2)}) async-start(), calls=%async_computation.4 | async-start | bytes 1179648
Sparse Core Ops, SparseCore 0:
  10.1 50.3 all-gather.3
  64.4 149.2 all-gather.5
  436.0 47.4 reduce-scatter.3
where the time goes:
time: 816 us; the launch traced here: 813 us
  waiting for transfers between devices  561 us (69%)
  local copies, waits for them, and re-layouts  121 us (15%)
  other arithmetic  58.1 us (7%)
  matrix products  46.1 us (6%)
  between operations  13.9 us (2%)
  starting transfers between devices  11 us (1%)
    all_to_all x1, waiting for transfers between devices, on_device(): lax.all_to_all(owner_grads, 'dp', split_axis=0, concat_axis=0, tiled=True)  365 us
    all_gather x1, waiting for transfers between devices, on_device(): arrived = lax.all_gather(stored, 'dp', axis=0, tiled=True)  152 us
    scatter-add x4, other arithmetic, step(): out_acc.at[:, part_cols]  47.4 us
    all_gather x1, waiting for transfers between devices, on_device(): full_grad = lax.all_gather(output_grad, 'tensor', axis=0, tiled=True)  43.7 us
    gather x8, local copies, waits for them, and re-layouts, step(): jnp.take(arrived, part_pos, axis=0)  37.9 us
    dynamic_update_slice x8, local copies, waits for them, and re-layouts, on_device(): lax.scan(step, start_acc, jnp.arange(turn_count, dtype=jnp.int32))  37.4 us
    dot_general x4, matrix products, step(): jnp.einsum('tgi,tgkj->gkij', part_hidden, chosen, preferred_element_type=...  16.4 us
  transfers between devices with their start and end apart: 4, of which 3 were waited for; matrix products, arithmetic and copies ran while one was open for 2% of the time, Pallas kernels for 0%

commit v1 on v0

v1 whole, which is shorter than its diff:
```python
import jax
import jax.numpy as jnp
import numpy as np
from jax import lax
from jax.experimental import pallas as pl
from jax.experimental.pallas import tpu as pltpu
from jax.sharding import Mesh, PartitionSpec as P

BLOCK = 64
HALF = 32
LANES = 128


def grads_kernel(cols, places, gate, up, grad, packed, wide):
    row_count, width = grad.shape
    kept = 16
    packed[...] = jnp.zeros_like(packed)

    def turn(pair, carry):
        columns = pl.ds(pl.multiple_of(pair * LANES, LANES), LANES)
        turned = grad[:, columns].T
        for side in range(2):
            for part in range(2):
                first = side * BLOCK + part * HALF
                wide[2 * pair + side, :, part * row_count : (part + 1) * row_count] = turned[
                    first : first + HALF
                ]
        return carry

    lax.fori_loop(0, width // LANES, turn, 0)
    lane = lax.broadcasted_iota(jnp.int32, (row_count, LANES), 1)

    def rows(pair, carry):
        columns = pl.ds(pl.multiple_of(pair * LANES, LANES), LANES)
        gate_wide = gate[:, columns].astype(jnp.float32)
        hidden = gate_wide * jax.nn.sigmoid(gate_wide) * up[:, columns].astype(jnp.float32)
        swapped = pltpu.roll(hidden, BLOCK, 1)
        for side in range(2):
            low, high = (hidden, swapped) if side == 0 else (swapped, hidden)
            spread = jnp.concatenate(
                [jnp.where(lane < BLOCK, low, 0.0), jnp.where(lane < BLOCK, 0.0, high)], axis=0
            ).astype(jnp.bfloat16)
            first = (2 * pair + side) * kept
            chosen = jnp.concatenate([wide[cols[first + k]] for k in range(kept)], axis=0)
            result = jnp.dot(chosen, spread, preferred_element_type=jnp.float32)
            result = result.astype(jnp.bfloat16)
            for k in range(kept):
                packed[places[first + k]] = result[k * HALF : (k + 1) * HALF]
        return carry

    lax.fori_loop(0, gate.shape[1] // LANES, rows, 0)


def passes_kernel(cols, places, gate, up, grad, blocks, out, gate_grad, up_grad, dense, hidden):
    row_count, width = grad.shape
    units = gate.shape[1]
    kept = 16
    lane = lax.broadcasted_iota(jnp.int32, (HALF, LANES), 1)

    def clear(step, carry):
        dense[pl.ds(pl.multiple_of(step * BLOCK, BLOCK), BLOCK), :] = jnp.zeros((BLOCK, units), jnp.bfloat16)
        return carry

    lax.fori_loop(0, width // BLOCK, clear, 0)

    def fill(pair, carry):
        columns = pl.ds(pl.multiple_of(pair * LANES, LANES), LANES)
        gate_wide = gate[:, columns].astype(jnp.float32)
        hidden[:, columns] = (
            gate_wide * jax.nn.sigmoid(gate_wide) * up[:, columns].astype(jnp.float32)
        ).astype(jnp.bfloat16)
        for side in range(2):
            mine = (lane < BLOCK) if side == 0 else (lane >= BLOCK)
            for k in range(kept):
                spot = (2 * pair + side) * kept + k
                block = blocks[places[spot]].astype(jnp.float32)
                swapped = pltpu.roll(block, BLOCK, 1)
                pieces = (block, swapped) if side == 0 else (swapped, block)
                first = cols[spot] * BLOCK
                for part in range(2):
                    there = pl.ds(pl.multiple_of(first + part * HALF, HALF), HALF)
                    old = dense[there, columns].astype(jnp.float32)
                    dense[there, columns] = jnp.where(mine, pieces[part], old).astype(jnp.bfloat16)
        return carry

    lax.fori_loop(0, units // LANES, fill, 0)
    step = 256

    def forward(turn, carry):
        columns = pl.ds(pl.multiple_of(turn * step, step), step)
        out[:, columns] = lax.dot_general(
            hidden[...], dense[columns, :], (((1,), (1,)), ((), ())), preferred_element_type=jnp.float32
        ).astype(out.dtype)
        return carry

    lax.fori_loop(0, width // step, forward, 0)

    def backward(turn, carry):
        columns = pl.ds(pl.multiple_of(turn * step, step), step)
        hidden_grad = jnp.dot(grad[...], dense[:, columns], preferred_element_type=jnp.float32)
        gate_wide = gate[:, columns].astype(jnp.float32)
        sigmoid_gate = jax.nn.sigmoid(gate_wide)
        up_grad[:, columns] = (hidden_grad * (gate_wide * sigmoid_gate)).astype(up_grad.dtype)
        gate_grad[:, columns] = (
            hidden_grad
            * up[:, columns].astype(jnp.float32)
            * sigmoid_gate
            * (1.0 + gate_wide * (1.0 - sigmoid_gate))
        ).astype(gate_grad.dtype)
        return carry

    lax.fori_loop(0, units // step, backward, 0)


def block_grads(cols, places, gate, up, grad, slots):
    rows, width = grad.shape
    return pl.pallas_call(
        grads_kernel,
        out_shape=jax.ShapeDtypeStruct((slots, HALF, LANES), jnp.bfloat16),
        grid_spec=pltpu.PrefetchScalarGridSpec(
            num_scalar_prefetch=2,
            grid=(),
            in_specs=[pl.BlockSpec(memory_space=pltpu.VMEM)] * 3,
            out_specs=pl.BlockSpec(memory_space=pltpu.VMEM),
            scratch_shapes=[pltpu.VMEM((width // BLOCK, HALF, 2 * rows), jnp.bfloat16)],
        ),
        compiler_params=pltpu.CompilerParams(vmem_limit_bytes=32 * 2**20),
        cost_estimate=pl.CostEstimate(flops=4 * 10**9, bytes_accessed=7 * 2**20, transcendentals=0),
        name="block_grads",
    )(cols, places, gate, up, grad)


def both_passes(cols, places, gate, up, grad, blocks):
    rows, width = grad.shape
    units = gate.shape[1]
    like = jax.ShapeDtypeStruct((rows, units), jnp.bfloat16)
    return pl.pallas_call(
        passes_kernel,
        out_shape=(jax.ShapeDtypeStruct((rows, width), jnp.bfloat16), like, like),
        grid_spec=pltpu.PrefetchScalarGridSpec(
            num_scalar_prefetch=2,
            grid=(),
            in_specs=[pl.BlockSpec(memory_space=pltpu.VMEM)] * 4,
            out_specs=[pl.BlockSpec(memory_space=pltpu.VMEM)] * 3,
            scratch_shapes=[
                pltpu.VMEM((width, units), jnp.bfloat16),
                pltpu.VMEM((rows, units), jnp.bfloat16),
            ],
        ),
        compiler_params=pltpu.CompilerParams(vmem_limit_bytes=48 * 2**20),
        cost_estimate=pl.CostEstimate(flops=4 * 10**9, bytes_accessed=8 * 2**20, transcendentals=0),
        name="both_passes",
    )(cols, places, gate, up, grad, blocks)


def swap(x, axis):
    return lax.ppermute(x, axis, [(0, 1), (1, 0)])


def on_device(gate_values, up_values, output_grad, kept_columns, block_owner, master_blocks):
    capacity, square = master_blocks.shape[2:]
    depth, flanks, cores = (lax.axis_size(name) for name in ("z", "x_hi", "core"))
    parts = lax.axis_size(("x_lo", "y"))
    slots = depth * flanks * cores * capacity
    row_count = output_grad.shape[0] * parts
    width = output_grad.shape[1]
    core, flank = lax.axis_index("core"), lax.axis_index("x_hi")

    stored = master_blocks.reshape(capacity, BLOCK, 2, HALF).astype(jnp.bfloat16)
    stored = stored.transpose(0, 3, 2, 1).reshape(capacity, HALF, LANES)
    beside = swap(stored, "x_hi")
    pair = jnp.where(flank == 0, jnp.stack([stored, beside]), jnp.stack([beside, stored]))
    column = lax.all_gather(pair, "z", axis=0, tiled=False)
    other = swap(column, "core")
    arrived = jnp.stack([column, other]).reshape(slots, HALF, LANES)

    full_grad = lax.all_to_all(
        jnp.broadcast_to(output_grad[None], (parts,) + output_grad.shape),
        ("x_lo", "y"), split_axis=0, concat_axis=0, tiled=True,
    ).reshape(row_count, width)

    owner = block_owner.reshape(-1)
    index = jnp.arange(owner.shape[0], dtype=jnp.int32)
    same = (owner[:, None] == owner[None, :]) & (index[None, :] < index[:, None])
    slot_rank = jnp.sum(same.astype(jnp.int32), axis=1)
    owner_core = owner % cores
    within = (owner // cores) * capacity + slot_rank
    half = slots // cores
    cols = kept_columns.reshape(-1)
    grads = block_grads(cols, owner_core * half + within, gate_values, up_values, full_grad, slots)
    grads = grads.reshape(cores, half, HALF, LANES)
    kept = lax.dynamic_index_in_dim(grads, core, 0, keepdims=False)
    sent = lax.dynamic_index_in_dim(grads, 1 - core, 0, keepdims=False)
    chip = (kept.astype(jnp.float32) + swap(sent, "core").astype(jnp.float32)).astype(jnp.bfloat16)
    chip = chip.reshape(depth, flanks, capacity, HALF, LANES)
    line = lax.psum_scatter(chip, "z", scatter_dimension=0, tiled=False)
    kept = lax.dynamic_index_in_dim(line, flank, 0, keepdims=False)
    sent = lax.dynamic_index_in_dim(line, 1 - flank, 0, keepdims=False)
    total = kept.astype(jnp.float32) + swap(sent, "x_hi").astype(jnp.float32)
    token_count = row_count * depth * flanks * cores
    total = total * float(token_count) ** (-0.5)
    master_grads = (
        total.reshape(capacity, HALF, 2, BLOCK).transpose(0, 3, 2, 1).reshape(1, 1, capacity, square)
    )

    here = (owner_core != core).astype(jnp.int32) * half + within
    partial_out, gate_grad, up_grad = both_passes(
        cols, here, gate_values, up_values, full_grad, arrived
    )
    shares = lax.all_to_all(
        partial_out.reshape(parts, row_count // parts, width),
        ("x_lo", "y"), split_axis=0, concat_axis=0, tiled=True,
    )
    layer_output = jnp.sum(shares.astype(jnp.float32), axis=0).astype(jnp.bfloat16)
    return layer_output, gate_grad, up_grad, master_grads


def solution(mesh):
    fine = Mesh(mesh.devices.reshape(16, 2, 2, 2, 4), ("z", "x_hi", "core", "x_lo", "y"))
    dp, tensor = ("z", "x_hi", "core"), ("x_lo", "y")
    return jax.shard_map(
        on_device,
        mesh=fine,
        in_specs=(
            P(dp, tensor),
            P(dp, tensor),
            P(dp + tensor, None),
            P(tensor, None),
            P(tensor, None),
            P(dp, tensor, None, None),
        ),
        out_specs=(
            P(dp + tensor, None),
            P(dp, tensor),
            P(dp, tensor),
            P(dp, tensor, None, None),
        ),
        check_vma=False,
    )
```

time: 816 us -> 187 us (0.23)
  waiting for transfers between devices: 561 us -> 98.4 us
  local copies, waits for them, and re-layouts: 121 us -> 8.1 us
  other arithmetic: 58.1 us -> 11.6 us
  matrix products: 46.1 us -> 0 us
  Pallas kernels: 0 us -> 30.6 us
  starting transfers between devices: 11 us -> 23.5 us
    all_to_all x1 -> x2, waiting for transfers between devices: 365 us -> 11.7 us  [the longest x1 11.7 us: on_device(): lax.all_to_all(jnp.broadcast_to(output_grad[None], (parts,) + output_grad...]
    all_gather x2 -> x1, waiting for transfers between devices: 195 us -> 34.8 us  [on_device(): column = lax.all_gather(pair, 'z', axis=0, tiled=False)]
    scatter-add x4 -> x0, other arithmetic: 47.4 us -> none  [step(): out_acc.at[:, part_cols]]
    gather x12 -> x0, local copies, waits for them, and re-layouts: 46.2 us -> none  [the longest x8 37.9 us: step(): jnp.take(arrived, part_pos, axis=0)]
    dot_general x12 -> x0, matrix products: 46.1 us -> none  [the longest x4 16.4 us: step(): jnp.einsum('tgi,tgkj->gkij', part_hidden, chosen, preferred_element_type=...]
    dynamic_update_slice x8 -> x0, local copies, waits for them, and re-layouts: 37.4 us -> none  [on_device(): lax.scan(step, start_acc, jnp.arange(turn_count, dtype=jnp.int32))]
    reduce_scatter x0 -> x1, waiting for transfers between devices: none -> 35.2 us  [on_device(): line = lax.psum_scatter(chip, 'z', scatter_dimension=0, tiled=False)]
    pallas_call x0 -> x2, Pallas kernels: none -> 30.6 us  [the longest x1 22 us: both_passes(): pl.pallas_call(passes_kernel, out_shape=(jax.ShapeDtypeStruct((rows, widt...]
  transfers between devices with their start and end apart: 4 -> 8, of which waited for: 3 -> 7; matrix products, arithmetic and copies ran while one was open for 2% -> 8% of each run, Pallas kernels for 0% -> 16%
where the time goes in v1:
time: 187 us; the launch traced here: 186 us
  waiting for transfers between devices  98.4 us (53%)
  Pallas kernels  30.6 us (16%)
  starting transfers between devices  23.5 us (13%)
  between operations  14.2 us (8%)
  other arithmetic  11.6 us (6%)
  local copies, waits for them, and re-layouts  8.1 us (4%)
    reduce_scatter x1, waiting for transfers between devices, on_device(): line = lax.psum_scatter(chip, 'z', scatter_dimension=0, tiled=False)  35.2 us
    all_gather x1, waiting for transfers between devices, on_device(): column = lax.all_gather(pair, 'z', axis=0, tiled=False)  34.8 us
    pallas_call x1, Pallas kernels, both_passes(): pl.pallas_call(passes_kernel, out_shape=(jax.ShapeDtypeStruct((rows, widt...  22 us
    ppermute x4, waiting for transfers between devices, swap(): return lax.ppermute(x, axis, [(0, 1), (1, 0)])  16.6 us
    all_to_all x1, waiting for transfers between devices, on_device(): lax.all_to_all(jnp.broadcast_to(output_grad[None], (parts,) + output_grad...  11.7 us
    ppermute x4, starting transfers between devices, swap(): return lax.ppermute(x, axis, [(0, 1), (1, 0)])  10.5 us
    pallas_call x1, Pallas kernels, block_grads(): pl.pallas_call(grads_kernel, out_shape=jax.ShapeDtypeStruct((slots, HALF,...  8.62 us
    all_to_all x1, starting transfers between devices, on_device(): lax.all_to_all(jnp.broadcast_to(output_grad[None], (parts,) + output_grad...  6.67 us
  transfers between devices with their start and end apart: 8, of which 7 were waited for; matrix products, arithmetic and copies ran while one was open for 8% of the time, Pallas kernels for 16%

profile of v1, /device:TPU:6, one launch (start us, length us, event | category | flops | bytes accessed | tf_op | source)
XLA Modules:
  0.0 186.3 jit_solution(5994903242894310315)
XLA Ops:
  7.2 0.9 convert_element_type.34
  8.1 0.2 convert_element_type.35
  8.3 0.1 copy.27
  8.5 0.1 reshape.113
  8.6 3.4 %collective-permute-start = (bf16[8,32,128]{2,1,0:T(8,128)(2,1)S(1)}, bf16[8,32,128]{2,1,0:T(8,128)(2,1)S(1)}, u32[]{:S(2)}, u32[]{:S(2)}) collective-permute-start(bf16[8,32,128]{2,1,0:T(8,128)(2,1)S(1)} %reshape.113), channel_id=1, source_target_pairs={{0,16},{16,0},{1,17},{17,1},{2,18},{18,2},{3,19},{19,3},{4,20},{20... | collective-permute-start | bytes 196616 | tf_op jit(solution)/shard_map/ppermute | solution.py:157
  12.2 4.2 %collective-permute-done = bf16[8,32,128]{2,1,0:T(8,128)(2,1)S(1)} collective-permute-done((bf16[8,32,128]{2,1,0:T(8,128)(2,1)S(1)}, bf16[8,32,128]{2,1,0:T(8,128)(2,1)S(1)}, u32[]{:S(2)}, u32[]{:S(2)}) %collective-permute-start) | collective-permute-done | bytes 65568 | tf_op jit(solution)/shard_map/ppermute | solution.py:157
  16.4 0.7 maximum_select_fusion
  17.1 2.0 %broadcast_in_dim.2 = bf16[8,16,4096]{2,1,0:T(8,128)(2,1)} broadcast(bf16[16,4096]{1,0:T(8,128)(2,1)} %param.8), dimensions={1,2} | broadcast | bytes 1179648 | tf_op jit(solution)/shard_map/broadcast_in_dim | solution.py:178
  19.1 6.7 %all-to-all-start = ((bf16[8,16,4096]{2,1,0:T(8,128)(2,1)}), bf16[8,16,4096]{2,1,0:T(8,128)(2,1)S(1)}, u32[]{:S(2)}, u32[]{:S(2)}) async-start(bf16[8,16,4096]{2,1,0:T(8,128)(2,1)} %broadcast_in_dim.2), calls=%async_computation | async-start | bytes 2097152 | tf_op jit(solution)/shard_map/all_to_all | solution.py:177
  26.1 0.3 convert_reduce_fusion
  26.4 11.7 %all-to-all-done = bf16[8,16,4096]{2,1,0:T(8,128)(2,1)S(1)} async-done(((bf16[8,16,4096]{2,1,0:T(8,128)(2,1)}), bf16[8,16,4096]{2,1,0:T(8,128)(2,1)S(1)}, u32[]{:S(2)}, u32[]{:S(2)}) %all-to-all-start) | async-done | bytes 1048608 | tf_op jit(solution)/shard_map/all_to_all | solution.py:177
  38.1 8.6 %block_grads.1 = bf16[512,32,128]{2,1,0:T(8,128)(2,1)S(1)} custom-call(s32[448]{0:T(512)S(1)} %reshape.110.cols, s32[448]{0:T(512)S(1)} %get-tuple-element.10.places, bf16[128,1792]{1,0:T(8,128)(2,1)S(1)} %copy-done.1, bf16[128,1792]{1,0:T(8,128)(2,1)S(1)} %copy-done.2, bf16[128,4096]{1,0:T(8,128)(2,1)S(1)} %bitcast.24), custom_call_target="tpu_custom_call" | custom-call | flops 4000000000 | bytes 7340032 | tf_op jit(solution)/shard_map/block_grads/pallas_call | solution.py:117
  46.8 2.0 %dynamic-slice_bitcast_fusion = bf16[256,32,128]{2,1,0:T(8,128)(2,1)} fusion(bf16[2,256,32,128]{3,2,1,0:T(8,128)(2,1)S(1)} %bitcast.22, s32[]{:T(128)S(6)} %select_n.46), kind=kLoop, calls=%fused_computation.3 | loop fusion | bytes 4194308 | tf_op jit(solution)/shard_map/jit(dynamic_index_in_dim)/squeeze | solution.py:193
  48.7 0.6 copy-done
  49.4 1.9 %collective-permute-start.2 = (bf16[256,32,128]{2,1,0:T(8,128)(2,1)}, bf16[256,32,128]{2,1,0:T(8,128)(2,1)}, u32[]{:S(2)}, u32[]{:S(2)}) collective-permute-start(bf16[256,32,128]{2,1,0:T(8,128)(2,1)} %dynamic-slice_bitcast_fusion), channel_id=1, source_target_pairs={{0,8},{8,0},{1,9},{9,1},{2,10},{10,2},{3,11},{11,3},{4,12},{12,4},... | collective-permute-start | bytes 6291464 | tf_op jit(solution)/shard_map/ppermute | solution.py:157
  51.3 4.5 %collective-permute-done.2 = bf16[256,32,128]{2,1,0:T(8,128)(2,1)} collective-permute-done((bf16[256,32,128]{2,1,0:T(8,128)(2,1)}, bf16[256,32,128]{2,1,0:T(8,128)(2,1)}, u32[]{:S(2)}, u32[]{:S(2)}) %collective-permute-start.2) | collective-permute-done | bytes 2097184 | tf_op jit(solution)/shard_map/ppermute | solution.py:157
  55.7 4.1 %fusion = bf16[256,32,128]{2,1,0:T(8,128)(2,1)} fusion(bf16[256,32,128]{2,1,0:T(8,128)(2,1)} %collective-permute-done.2, bf16[2,256,32,128]{3,2,1,0:T(8,128)(2,1)} %bitcast.23, s32[]{:T(128)S(6)} %select_n.45), kind=kLoop, calls=%fused_computation.2 | loop fusion | flops 4194304 | bytes 6291460 | tf_op jit(solution)/shard_map/convert_element_type | solution.py:194
  59.9 34.8 %all-gather.2.cloned.1.call-done = bf16[16,2,8,32,128]{4,3,2,1,0:T(8,128)(2,1)} async-done(((bf16[1,2,8,32,128]{4,3,2,1,0:T(8,128)(2,1)}), bf16[16,2,8,32,128]{4,3,2,1,0:T(8,128)(2,1)}) %all-gather.2.cloned.1.call-update) | async-done | bytes 2097168 | tf_op jit(solution)/shard_map/all_gather | solution.py:173
  94.6 1.9 %collective-permute-start.1 = (bf16[16,2,8,32,128]{4,3,2,1,0:T(8,128)(2,1)}, bf16[16,2,8,32,128]{4,3,2,1,0:T(8,128)(2,1)S(1)}, u32[]{:S(2)}, u32[]{:S(2)}) collective-permute-start(bf16[16,2,8,32,128]{4,3,2,1,0:T(8,128)(2,1)} %all-gather.2.cloned.1.call-done), channel_id=1, source_target_pairs={{0,8},{8,0},{1,9},{9,1},{2,10},{10,2},{3,11},{11,3},{4,12},{12,4},... | collective-permute-start | bytes 6291464 | tf_op jit(solution)/shard_map/ppermute | solution.py:157
  96.6 4.3 %collective-permute-done.1 = bf16[16,2,8,32,128]{4,3,2,1,0:T(8,128)(2,1)S(1)} collective-permute-done((bf16[16,2,8,32,128]{4,3,2,1,0:T(8,128)(2,1)}, bf16[16,2,8,32,128]{4,3,2,1,0:T(8,128)(2,1)S(1)}, u32[]{:S(2)}, u32[]{:S(2)}) %collective-permute-start.1) | collective-permute-done | bytes 2097184 | tf_op jit(solution)/shard_map/ppermute | solution.py:157
  100.9 3.9 %pad_maximum_fusion = bf16[2,16,2,8,32,128]{5,4,3,2,1,0:T(8,128)(2,1)} fusion(bf16[1,16,2,8,32,128]{5,4,3,2,1,0:T(8,128)(2,1)S(1)} %bitcast.29, bf16[1,16,2,8,32,128]{5,4,3,2,1,0:T(8,128)(2,1)} %bitcast.28), kind=kLoop, calls=%fused_computation | loop fusion | flops 2097152 | bytes 8388608 | tf_op jit(solution)/shard_map/stack | solution.py:175
  104.8 22.0 %both_passes.1 = (bf16[128,4096]{1,0:T(8,128)(2,1)}, bf16[128,1792]{1,0:T(8,128)(2,1)}, bf16[128,1792]{1,0:T(8,128)(2,1)}) custom-call(s32[448]{0:T(512)S(1)} %reshape.110.cols, s32[448]{0:T(512)S(1)} %select_add_fusion.places, bf16[128,1792]{1,0:T(8,128)(2,1)S(1)} %copy-done.1, bf16[128,1792]{1,0:T(8,128)(2,1)S(1)} %copy-done.2, ...), custom_call_target="tpu_custom_call" | custom-call | flops 4000000000 | bytes 8388608 | tf_op jit(solution)/shard_map/both_passes/pallas_call | solution.py:137
  126.8 6.3 %all-to-all-start.1 = ((bf16[8,16,4096]{2,1,0:T(8,128)(2,1)}), bf16[8,16,4096]{2,1,0:T(8,128)(2,1)S(1)}, u32[]{:S(2)}, u32[]{:S(2)}) async-start(bf16[8,16,4096]{2,1,0:T(8,128)(2,1)} %bitcast.6), calls=%async_computation.1 | async-start | bytes 2097152 | tf_op jit(solution)/shard_map/all_to_all | solution.py:210
  133.1 35.2 %reduce-scatter.2.cloned.1.call-done = bf16[1,2,8,32,128]{4,3,2,1,0:T(8,128)(2,1)} async-done(((bf16[16,2,8,32,128]{4,3,2,1,0:T(8,128)(2,1)}), bf16[1,2,8,32,128]{4,3,2,1,0:T(8,128)(2,1)}) %reduce-scatter.2.cloned.1.call-update) | async-done | bytes 131088 | tf_op jit(solution)/shard_map/reduce_scatter | solution.py:196
  168.3 0.8 dynamic-slice_bitcast_fusion.1
  169.2 3.2 %collective-permute-start.3 = (bf16[8,32,128]{2,1,0:T(8,128)(2,1)S(1)}, bf16[8,32,128]{2,1,0:T(8,128)(2,1)S(1)}, u32[]{:S(2)}, u32[]{:S(2)}) collective-permute-start(bf16[8,32,128]{2,1,0:T(8,128)(2,1)S(1)} %dynamic-slice_bitcast_fusion.1), channel_id=1, source_target_pairs={{0,16},{16,0},{1,17},{17,1},{2,18},{18,2},{3,19},{19,3},{4,20},{20... | collective-permute-start | bytes 196616 | tf_op jit(solution)/shard_map/ppermute | solution.py:157
  172.4 0.8 reduce_sum.22
  173.2 3.6 %collective-permute-done.3 = bf16[8,32,128]{2,1,0:T(8,128)(2,1)S(1)} collective-permute-done((bf16[8,32,128]{2,1,0:T(8,128)(2,1)S(1)}, bf16[8,32,128]{2,1,0:T(8,128)(2,1)S(1)}, u32[]{:S(2)}, u32[]{:S(2)}) %collective-permute-start.3) | collective-permute-done | bytes 65568 | tf_op jit(solution)/shard_map/ppermute | solution.py:157
  176.8 0.9 fusion.2
  177.7 0.2 reshape.118
  177.9 0.3 copy.29
  178.1 1.3 reshape.119
  (21 shorter events, 0.6 us)
Async XLA Ops:
  7.2 87.5 %all-gather.2.cloned.1.call-start = ((), (), s32[]{:S(2)}) async-start(), calls=%async_computation.3 | async-start | bytes 2228224 | tf_op jit(solution)/shard_map/all_gather | solution.py:173
  8.5 17.3 %copy-start.3 = (s32[28,16]{0,1:T(8,128)S(1)}, s32[28,16]{0,1:T(8,128)}, u32[]{:S(2)}) copy-start(s32[28,16]{0,1:T(8,128)} %param.9) | copy-start | bytes 5380
  8.5 17.5 %copy-start.4 = (s32[28,16]{0,1:T(8,128)S(1)}, s32[28,16]{0,1:T(8,128)}, u32[]{:S(2)}) copy-start(s32[28,16]{0,1:T(8,128)} %param.10) | copy-start | bytes 5380
  8.5 29.6 %copy-start.1 = (bf16[128,1792]{1,0:T(8,128)(2,1)S(1)}, bf16[128,1792]{1,0:T(8,128)(2,1)}, u32[]{:S(2)}) copy-start(bf16[128,1792]{1,0:T(8,128)(2,1)} %gate.3) | copy-start | bytes 1376260
  8.5 29.6 %copy-start.2 = (bf16[128,1792]{1,0:T(8,128)(2,1)S(1)}, bf16[128,1792]{1,0:T(8,128)(2,1)}, u32[]{:S(2)}) copy-start(bf16[128,1792]{1,0:T(8,128)(2,1)} %up.3) | copy-start | bytes 1376260
  8.6 7.8 %collective-permute-start = (bf16[8,32,128]{2,1,0:T(8,128)(2,1)S(1)}, bf16[8,32,128]{2,1,0:T(8,128)(2,1)S(1)}, u32[]{:S(2)}, u32[]{:S(2)}) collective-permute-start(bf16[8,32,128]{2,1,0:T(8,128)(2,1)S(1)} %reshape.113), channel_id=1, source_target_pairs={{0,16},{16,0},{1,17},{17,1},{2,18},{18,2},{3,19},{19,3},{4,20},{20... | collective-permute-start | bytes 196616 | tf_op jit(solution)/shard_map/ppermute | solution.py:157
  19.1 19.0 %all-to-all-start = ((bf16[8,16,4096]{2,1,0:T(8,128)(2,1)}), bf16[8,16,4096]{2,1,0:T(8,128)(2,1)S(1)}, u32[]{:S(2)}, u32[]{:S(2)}) async-start(bf16[8,16,4096]{2,1,0:T(8,128)(2,1)} %broadcast_in_dim.2), calls=%async_computation | async-start | bytes 2097152 | tf_op jit(solution)/shard_map/all_to_all | solution.py:177
  25.8 142.5 %reduce-scatter.2.cloned.1.call-start = ((), (), s32[]{:S(2)}) async-start(), calls=%async_computation.4 | async-start | bytes 2228224 | tf_op jit(solution)/shard_map/reduce_scatter | solution.py:196
  46.8 2.6 %copy-start = (bf16[512,32,128]{2,1,0:T(8,128)(2,1)}, bf16[512,32,128]{2,1,0:T(8,128)(2,1)S(1)}, u32[]{:S(2)}) copy-start(bf16[512,32,128]{2,1,0:T(8,128)(2,1)S(1)} %block_grads.1) | copy-start | bytes 12582916
  49.4 6.4 %collective-permute-start.2 = (bf16[256,32,128]{2,1,0:T(8,128)(2,1)}, bf16[256,32,128]{2,1,0:T(8,128)(2,1)}, u32[]{:S(2)}, u32[]{:S(2)}) collective-permute-start(bf16[256,32,128]{2,1,0:T(8,128)(2,1)} %dynamic-slice_bitcast_fusion), channel_id=1, source_target_pairs={{0,8},{8,0},{1,9},{9,1},{2,10},{10,2},{3,11},{11,3},{4,12},{12,4},... | collective-permute-start | bytes 6291464 | tf_op jit(solution)/shard_map/ppermute | solution.py:157
  94.6 6.3 %collective-permute-start.1 = (bf16[16,2,8,32,128]{4,3,2,1,0:T(8,128)(2,1)}, bf16[16,2,8,32,128]{4,3,2,1,0:T(8,128)(2,1)S(1)}, u32[]{:S(2)}, u32[]{:S(2)}) collective-permute-start(bf16[16,2,8,32,128]{4,3,2,1,0:T(8,128)(2,1)} %all-gather.2.cloned.1.call-done), channel_id=1, source_target_pairs={{0,8},{8,0},{1,9},{9,1},{2,10},{10,2},{3,11},{11,3},{4,12},{12,4},... | collective-permute-start | bytes 6291464 | tf_op jit(solution)/shard_map/ppermute | solution.py:157
  126.8 45.6 %all-to-all-start.1 = ((bf16[8,16,4096]{2,1,0:T(8,128)(2,1)}), bf16[8,16,4096]{2,1,0:T(8,128)(2,1)S(1)}, u32[]{:S(2)}, u32[]{:S(2)}) async-start(bf16[8,16,4096]{2,1,0:T(8,128)(2,1)} %bitcast.6), calls=%async_computation.1 | async-start | bytes 2097152 | tf_op jit(solution)/shard_map/all_to_all | solution.py:210
  169.2 7.7 %collective-permute-start.3 = (bf16[8,32,128]{2,1,0:T(8,128)(2,1)S(1)}, bf16[8,32,128]{2,1,0:T(8,128)(2,1)S(1)}, u32[]{:S(2)}, u32[]{:S(2)}) collective-permute-start(bf16[8,32,128]{2,1,0:T(8,128)(2,1)S(1)} %dynamic-slice_bitcast_fusion.1), channel_id=1, source_target_pairs={{0,16},{16,0},{1,17},{17,1},{2,18},{18,2},{3,19},{19,3},{4,20},{20... | collective-permute-start | bytes 196616 | tf_op jit(solution)/shard_map/ppermute | solution.py:157
Sparse Core Ops, SparseCore 0:
  17.2 77.3 all-gather.1
  97.5 70.8 reduce-scatter.1

commit v2 on v1

v2 whole, which is shorter than its diff:
```python
import jax
import jax.numpy as jnp
import numpy as np
from jax import lax
from jax.experimental import pallas as pl
from jax.experimental.pallas import tpu as pltpu
from jax.sharding import Mesh, PartitionSpec as P

BLOCK = 64
HALF = 32
LANES = 128
Z = ("z_hi", "z_lo")


def grads_kernel(cols, places, gate_far, up_far, grad, packed, wide, gate, up, arrivals):
    row_count, width = grad.shape
    kept = 16
    copies = [
        pltpu.make_async_copy(gate_far, gate, arrivals.at[0]),
        pltpu.make_async_copy(up_far, up, arrivals.at[1]),
    ]
    for copy in copies:
        copy.start()
    packed[...] = jnp.zeros_like(packed)

    def turn(pair, carry):
        columns = pl.ds(pl.multiple_of(pair * LANES, LANES), LANES)
        turned = grad[:, columns].T
        for side in range(2):
            for part in range(2):
                first = side * BLOCK + part * HALF
                wide[2 * pair + side, :, part * row_count : (part + 1) * row_count] = turned[
                    first : first + HALF
                ]
        return carry

    lax.fori_loop(0, width // LANES, turn, 0, unroll=32)
    for copy in copies:
        copy.wait()
    lane = lax.broadcasted_iota(jnp.int32, (row_count, LANES), 1)

    def rows(pair, carry):
        columns = pl.ds(pl.multiple_of(pair * LANES, LANES), LANES)
        gate_wide = gate[:, columns].astype(jnp.float32)
        hidden = gate_wide * jax.nn.sigmoid(gate_wide) * up[:, columns].astype(jnp.float32)
        swapped = pltpu.roll(hidden, BLOCK, 1)
        for side in range(2):
            low, high = (hidden, swapped) if side == 0 else (swapped, hidden)
            spread = jnp.concatenate(
                [jnp.where(lane < BLOCK, low, 0.0), jnp.where(lane < BLOCK, 0.0, high)], axis=0
            ).astype(jnp.bfloat16)
            first = (2 * pair + side) * kept
            chosen = jnp.concatenate([wide[cols[first + k]] for k in range(kept)], axis=0)
            result = jnp.dot(chosen, spread, preferred_element_type=jnp.float32)
            result = result.astype(jnp.bfloat16)
            for k in range(kept):
                packed[places[first + k]] = result[k * HALF : (k + 1) * HALF]
        return carry

    lax.fori_loop(0, gate.shape[1] // LANES, rows, 0, unroll=14)


def passes_kernel(
    cols, places, gate, up, wide, *refs
):
    *pieces, out, gate_grad, up_grad, sums, blocks, arrivals = refs
    row_count = gate.shape[0]
    kept = 16
    copies, first = [], 0
    for index, piece in enumerate(pieces):
        there = blocks.at[pl.ds(first, piece.shape[0])]
        copies.append(pltpu.make_async_copy(piece, there, arrivals.at[index]))
        first += piece.shape[0]
    for copy in copies:
        copy.start()

    def clear(index, carry):
        sums[index] = jnp.zeros(sums.shape[1:], jnp.float32)
        return carry

    lax.fori_loop(0, sums.shape[0], clear, 0, unroll=8)
    for copy in copies:
        copy.wait()
    empty = jnp.zeros((BLOCK, row_count), jnp.bfloat16)

    def rows(pair, carry):
        columns = pl.ds(pl.multiple_of(pair * LANES, LANES), LANES)
        gate_wide = gate[:, columns].astype(jnp.float32)
        up_wide = up[:, columns].astype(jnp.float32)
        sigmoid_gate = jax.nn.sigmoid(gate_wide)
        swish_gate = gate_wide * sigmoid_gate
        turned = (swish_gate * up_wide).T.astype(jnp.bfloat16)
        halves = []
        for side in range(2):
            mine = turned[side * BLOCK : (side + 1) * BLOCK]
            spread = jnp.concatenate(
                [jnp.concatenate([mine, empty], axis=1), jnp.concatenate([empty, mine], axis=1)], axis=0
            )
            first = (2 * pair + side) * kept
            weights = jnp.concatenate([blocks[places[first + k]] for k in range(kept)], axis=0)
            forward = jnp.dot(weights, spread, preferred_element_type=jnp.float32)
            for start in range(0, kept, 4):
                group = range(start, start + 4)
                old = [sums[cols[first + k]] for k in group]
                for k in group:
                    sums[cols[first + k]] = old[k - start] + forward[k * HALF : (k + 1) * HALF]
            chosen = jnp.concatenate([wide[cols[first + k]] for k in range(kept)], axis=0)
            backward = lax.dot_general(
                weights, chosen, (((0,), (0,)), ((), ())), preferred_element_type=jnp.float32
            )
            halves.append(backward[:BLOCK, :row_count] + backward[BLOCK:, row_count:])
        hidden_grad = jnp.concatenate(halves, axis=0).T
        up_grad[:, columns] = (hidden_grad * swish_gate).astype(up_grad.dtype)
        gate_grad[:, columns] = (
            hidden_grad * up_wide * sigmoid_gate * (1.0 + gate_wide * (1.0 - sigmoid_gate))
        ).astype(gate_grad.dtype)
        return carry

    lax.fori_loop(0, gate.shape[1] // LANES, rows, 0, unroll=14)

    def close(pair, carry):
        columns = pl.ds(pl.multiple_of(pair * LANES, LANES), LANES)
        tall = jnp.concatenate(
            [
                sums[2 * pair + side][:, part * row_count : (part + 1) * row_count]
                for side in range(2)
                for part in range(2)
            ],
            axis=0,
        )
        out[:, columns] = tall.T.astype(out.dtype)
        return carry

    lax.fori_loop(0, sums.shape[0] // 2, close, 0, unroll=32)


def block_grads(cols, places, gate, up, grad, slots):
    rows, width = grad.shape
    return pl.pallas_call(
        grads_kernel,
        out_shape=(
            jax.ShapeDtypeStruct((slots, HALF, LANES), jnp.bfloat16),
            jax.ShapeDtypeStruct((width // BLOCK, HALF, 2 * rows), jnp.bfloat16),
        ),
        grid_spec=pltpu.PrefetchScalarGridSpec(
            num_scalar_prefetch=2,
            grid=(),
            in_specs=[pl.BlockSpec(memory_space=pl.ANY)] * 2 + [pl.BlockSpec(memory_space=pltpu.VMEM)],
            out_specs=[pl.BlockSpec(memory_space=pltpu.VMEM)] * 2,
            scratch_shapes=[pltpu.VMEM(gate.shape, gate.dtype), pltpu.VMEM(up.shape, up.dtype), pltpu.SemaphoreType.DMA((2,))],
        ),
        compiler_params=pltpu.CompilerParams(vmem_limit_bytes=32 * 2**20),
        cost_estimate=pl.CostEstimate(flops=9 * 10**9, bytes_accessed=7 * 2**20, transcendentals=0),
        name="block_grads",
    )(cols, places, gate, up, grad)


def both_passes(cols, places, gate, up, wide, *pieces):
    rows, units = gate.shape
    col_blocks = wide.shape[0]
    like = jax.ShapeDtypeStruct((rows, units), jnp.bfloat16)
    return pl.pallas_call(
        passes_kernel,
        out_shape=(jax.ShapeDtypeStruct((rows, col_blocks * BLOCK), jnp.bfloat16), like, like),
        grid_spec=pltpu.PrefetchScalarGridSpec(
            num_scalar_prefetch=2,
            grid=(),
            in_specs=[pl.BlockSpec(memory_space=pltpu.VMEM)] * 3 + [pl.BlockSpec(memory_space=pl.ANY)] * len(pieces),
            out_specs=[pl.BlockSpec(memory_space=pltpu.VMEM)] * 3,
            scratch_shapes=[
                pltpu.VMEM((col_blocks, HALF, 2 * rows), jnp.float32),
                pltpu.VMEM((sum(piece.shape[0] for piece in pieces), HALF, LANES), jnp.bfloat16),
                pltpu.SemaphoreType.DMA((len(pieces),)),
            ],
        ),
        compiler_params=pltpu.CompilerParams(vmem_limit_bytes=32 * 2**20),
        cost_estimate=pl.CostEstimate(flops=10**6, bytes_accessed=2**16, transcendentals=0),
        name="both_passes",
    )(cols, places, gate, up, wide, *pieces)


def swap(x, axis):
    return lax.ppermute(x, axis, [(0, 1), (1, 0)])


def after(x, *others):
    return lax.optimization_barrier((x,) + others)[0]


def add_up(x, y):
    return (x.astype(jnp.float32) + y.astype(jnp.float32)).astype(jnp.bfloat16)


def on_device(gate_values, up_values, output_grad, kept_columns, block_owner, master_blocks):
    capacity, square = master_blocks.shape[2:]
    depth, flanks, cores = (lax.axis_size(name) for name in (Z, "x_hi", "core"))
    parts = lax.axis_size(("x_lo", "y"))
    slots = depth * flanks * cores * capacity
    row_count = output_grad.shape[0] * parts
    width = output_grad.shape[1]
    core, flank = lax.axis_index("core"), lax.axis_index("x_hi")

    stored = master_blocks.reshape(capacity, BLOCK, 2, HALF).astype(jnp.bfloat16)
    stored = stored.transpose(0, 3, 2, 1).reshape(capacity, HALF, LANES)
    copies = jnp.broadcast_to(output_grad[None], (parts,) + output_grad.shape)
    full_grad = lax.all_to_all(
        copies, ("x_lo", "y"), split_axis=0, concat_axis=0, tiled=True
    ).reshape(row_count, width)
    stored = after(stored, copies)
    away = depth // 2
    across = [((z * 2 + x), ((z + away) % depth) * 2 + 1 - x) for z in range(depth) for x in range(2)]
    shift = lambda x, by: lax.ppermute(x, Z, [(z, (z + by) % depth) for z in range(depth)])
    firsts = [stored, swap(stored, "x_hi"), shift(stored, away), lax.ppermute(stored, Z + ("x_hi",), across)]
    own = jnp.concatenate(firsts)

    owner = block_owner.reshape(-1)
    index = jnp.arange(owner.shape[0], dtype=jnp.int32)
    same = (owner[:, None] == owner[None, :]) & (index[None, :] < index[:, None])
    slot_rank = jnp.sum(same.astype(jnp.int32), axis=1)
    owner_core = owner % cores
    owner_flank = (owner // cores) % flanks
    owner_depth = owner // (cores * flanks)
    far_core = (owner_core != core).astype(jnp.int32)
    far_flank = (owner_flank != flank).astype(jnp.int32)
    cols = kept_columns.reshape(-1)
    spots = ((far_core * depth + owner_depth) * flanks + far_flank) * capacity + slot_rank
    grads, wide = block_grads(cols, spots, gate_values, up_values, after(full_grad, *firsts), slots)
    grads = grads.reshape(cores, depth, flanks, capacity, HALF, LANES)
    chip = add_up(grads[0], swap(grads[1], "core"))
    line = lax.psum_scatter(chip, Z, scatter_dimension=0, tiled=False)
    total = line[0].astype(jnp.float32) + swap(line[1], "x_hi").astype(jnp.float32)
    own = after(own, chip)
    ups, downs, rise, fall = [], [], own, own
    for hop in range(1, away // 2):
        rise, fall = shift(rise, -1), shift(fall, 1)
        ups.append(rise)
        downs.append(fall)
    last = 2 * capacity
    near = jnp.concatenate([own] + ups + downs + [shift(rise[:last], -1), shift(fall[:last], 1)])
    far = swap(near, "core")
    ahead = (owner_depth - lax.axis_index(Z)) % depth
    ahead_slot = [0] * depth
    for hop in range(1, away // 2):
        ahead_slot[hop], ahead_slot[hop + away] = 4 * hop, 4 * hop + 2
        back = 4 * (away // 2 - 1 + hop)
        ahead_slot[depth - hop], ahead_slot[away - hop] = back, back + 2
    ahead_slot[away] = 2
    ahead_slot[away // 2] = 4 * (away - 1)
    ahead_slot[depth - away // 2] = 4 * (away - 1) + 2
    piece = jnp.asarray(np.array(ahead_slot, np.int32))[ahead] + far_flank
    here = far_core * (depth * flanks * capacity) + piece * capacity + slot_rank
    token_count = row_count * depth * flanks * cores
    total = total * float(token_count) ** (-0.5)
    master_grads = (
        total.reshape(capacity, HALF, 2, BLOCK).transpose(0, 3, 2, 1).reshape(1, 1, capacity, square)
    )
    partial_out, gate_grad, up_grad = both_passes(
        cols, here, gate_values, up_values, wide, near, far
    )
    shares = lax.all_to_all(
        partial_out.reshape(parts, row_count // parts, width),
        ("x_lo", "y"), split_axis=0, concat_axis=0, tiled=True,
    )
    layer_output = jnp.sum(shares.astype(jnp.float32), axis=0).astype(jnp.bfloat16)
    return layer_output, gate_grad, up_grad, master_grads


def solution(mesh):
    fine = Mesh(mesh.devices.reshape(4, 4, 2, 2, 2, 4), ("z_hi", "z_lo", "x_hi", "core", "x_lo", "y"))
    dp, tensor = Z + ("x_hi", "core"), ("x_lo", "y")
    return jax.shard_map(
        on_device,
        mesh=fine,
        in_specs=(
            P(dp, tensor),
            P(dp, tensor),
            P(dp + tensor, None),
            P(tensor, None),
            P(tensor, None),
            P(dp, tensor, None, None),
        ),
        out_specs=(
            P(dp + tensor, None),
            P(dp, tensor),
            P(dp, tensor),
            P(dp, tensor, None, None),
        ),
        check_vma=False,
    )
```

time: 187 us -> 158 us (0.84)
  waiting for transfers between devices: 98.4 us -> 50.2 us
  starting transfers between devices: 23.5 us -> 71 us
  Pallas kernels: 30.6 us -> 10.8 us
  other arithmetic: 11.6 us -> 4.22 us
    ppermute x0 -> x10, starting transfers between devices: none -> 48.3 us  [the longest x9 31.7 us: on_device(): lax.ppermute(x, Z, [(z, (z + by) % depth) for z in range(depth)])]
    all_gather x1 -> x0, waiting for transfers between devices: 34.8 us -> none  [on_device(): column = lax.all_gather(pair, 'z', axis=0, tiled=False)]
    ppermute x0 -> x10, waiting for transfers between devices: none -> 26.2 us  [the longest x9 26.1 us: on_device(): lax.ppermute(x, Z, [(z, (z + by) % depth) for z in range(depth)])]
    reduce_scatter x1, waiting for transfers between devices: 35.2 us -> 12.6 us  [on_device(): line = lax.psum_scatter(chip, Z, scatter_dimension=0, tiled=False)]
    pallas_call x2, Pallas kernels: 30.6 us -> 10.8 us  [the longest x1 6.61 us: both_passes(): pl.pallas_call(passes_kernel, out_shape=(jax.ShapeDtypeStruct((rows, col_...]
    all_to_all x1, waiting for transfers between devices: 11.7 us -> 0.01 us  [on_device(): lax.all_to_all(copies, ('x_lo', 'y'), split_axis=0, concat_axis=0, tiled=...]
    ppermute x4, waiting for transfers between devices: 16.6 us -> 11.4 us  [swap(): return lax.ppermute(x, axis, [(0, 1), (1, 0)])]
    another operation x1 -> x0, other arithmetic: 3.92 us -> none  [on_device(): arrived = jnp.stack([column, other]).reshape(slots, HALF, LANES)]
  transfers between devices with their start and end apart: 8 -> 17, of which waited for: 7 -> 11; matrix products, arithmetic and copies ran while one was open for 8% -> 2% of each run, Pallas kernels for 16% -> 4%
where the time goes in v2:
time: 158 us; the launch traced here: 157 us
  starting transfers between devices  71 us (45%)
  waiting for transfers between devices  50.2 us (32%)
  between operations  14.4 us (9%)
  Pallas kernels  10.8 us (7%)
  local copies, waits for them, and re-layouts  6.6 us (4%)
  other arithmetic  4.22 us (3%)
    ppermute x9, starting transfers between devices, on_device(): lax.ppermute(x, Z, [(z, (z + by) % depth) for z in range(depth)])  31.7 us
    ppermute x9, waiting for transfers between devices, on_device(): lax.ppermute(x, Z, [(z, (z + by) % depth) for z in range(depth)])  26.1 us
    ppermute x1, starting transfers between devices, on_device(): lax.ppermute(stored, Z + ('x_hi',), across)  16.6 us
    reduce_scatter x1, waiting for transfers between devices, on_device(): line = lax.psum_scatter(chip, Z, scatter_dimension=0, tiled=False)  12.6 us
    ppermute x4, waiting for transfers between devices, swap(): return lax.ppermute(x, axis, [(0, 1), (1, 0)])  11.4 us
    ppermute x4, starting transfers between devices, swap(): return lax.ppermute(x, axis, [(0, 1), (1, 0)])  11.1 us
    pallas_call x1, Pallas kernels, both_passes(): pl.pallas_call(passes_kernel, out_shape=(jax.ShapeDtypeStruct((rows, col_...  6.61 us
    all_to_all x1, starting transfers between devices, on_device(): lax.all_to_all(copies, ('x_lo', 'y'), split_axis=0, concat_axis=0, tiled=...  5.93 us
  transfers between devices with their start and end apart: 17, of which 11 were waited for; matrix products, arithmetic and copies ran while one was open for 2% of the time, Pallas kernels for 4%

profile of v2, /device:TPU:6, one launch (start us, length us, event | category | flops | bytes accessed | tf_op | source)
XLA Modules:
  0.0 157.3 jit_solution(782940151168235150)
XLA Ops:
  7.2 2.1 %broadcast_in_dim.2 = bf16[8,16,4096]{2,1,0:T(8,128)(2,1)} broadcast(bf16[16,4096]{1,0:T(8,128)(2,1)} %param.9), dimensions={1,2} | broadcast | bytes 1179648 | tf_op jit(solution)/shard_map/broadcast_in_dim | solution.py:205
  9.3 5.9 %all-to-all-start = ((bf16[8,16,4096]{2,1,0:T(8,128)(2,1)}), bf16[8,16,4096]{2,1,0:T(8,128)(2,1)S(1)}, u32[]{:S(2)}, u32[]{:S(2)}) async-start(bf16[8,16,4096]{2,1,0:T(8,128)(2,1)} %broadcast_in_dim.2), calls=%async_computation | async-start | bytes 2097152 | tf_op jit(solution)/shard_map/all_to_all | solution.py:206
  15.7 16.6 %collective-permute-start.2 = (bf16[8,32,128]{2,1,0:T(8,128)(2,1)S(1)}, bf16[8,32,128]{2,1,0:T(8,128)(2,1)S(1)}, u32[]{:S(2)}, u32[]{:S(2)}) collective-permute-start(bf16[8,32,128]{2,1,0:T(8,128)(2,1)S(1)} %reshape.168), channel_id=1, source_target_pairs={{0,272},{16,256},{32,304},{48,288},{64,336},{80,320},{96,368},{112... | collective-permute-start | bytes 196616 | tf_op jit(solution)/shard_map/ppermute | solution.py:213
  32.3 2.3 %collective-permute-start.1 = (bf16[8,32,128]{2,1,0:T(8,128)(2,1)S(1)}, bf16[8,32,128]{2,1,0:T(8,128)(2,1)S(1)}, u32[]{:S(2)}, u32[]{:S(2)}) collective-permute-start(bf16[8,32,128]{2,1,0:T(8,128)(2,1)S(1)} %reshape.168), channel_id=1, source_target_pairs={{0,256},{32,288},{64,320},{96,352},{128,384},{160,416},{192,448},{... | collective-permute-start | bytes 196616 | tf_op jit(solution)/shard_map/ppermute | solution.py:212
  34.6 3.7 %collective-permute-start = (bf16[8,32,128]{2,1,0:T(8,128)(2,1)S(1)}, bf16[8,32,128]{2,1,0:T(8,128)(2,1)S(1)}, u32[]{:S(2)}, u32[]{:S(2)}) collective-permute-start(bf16[8,32,128]{2,1,0:T(8,128)(2,1)S(1)} %reshape.168), channel_id=1, source_target_pairs={{0,16},{16,0},{1,17},{17,1},{2,18},{18,2},{3,19},{19,3},{4,20},{20... | collective-permute-start | bytes 196616 | tf_op jit(solution)/shard_map/ppermute | solution.py:183
  39.1 8.2 %collective-permute-done.1 = bf16[8,32,128]{2,1,0:T(8,128)(2,1)S(1)} collective-permute-done((bf16[8,32,128]{2,1,0:T(8,128)(2,1)S(1)}, bf16[8,32,128]{2,1,0:T(8,128)(2,1)S(1)}, u32[]{:S(2)}, u32[]{:S(2)}) %collective-permute-start.1) | collective-permute-done | bytes 65568 | tf_op jit(solution)/shard_map/ppermute | solution.py:212
  47.3 4.2 %block_grads.1 = (bf16[512,32,128]{2,1,0:T(8,128)(2,1)S(1)}, bf16[64,32,256]{2,1,0:T(8,128)(2,1)S(1)}) custom-call(s32[448]{0:T(512)S(1)} %reshape.164.cols, s32[448]{0:T(512)S(1)} %get-tuple-element.33.places, bf16[128,1792]{1,0:T(8,128)(2,1)S(1)} %copy-done, bf16[128,1792]{1,0:T(8,128)(2,1)S(1)} %copy-done.1, bf16[128,4096]{1,0:T(8,128)(2,1)S(1)} %bitcast.17), custom_call_target="tpu_custom_call" | custom-call | flops 8999999488 | bytes 7340032 | tf_op jit(solution)/shard_map/block_grads/pallas_call | solution.py:139
  52.2 1.9 %collective-permute-start.3 = (bf16[16,2,8,32,128]{4,3,2,1,0:T(8,128)(2,1)S(1)}, bf16[16,2,8,32,128]{4,3,2,1,0:T(8,128)(2,1)S(1)}, u32[]{:S(2)}, u32[]{:S(2)}) collective-permute-start(bf16[16,2,8,32,128]{4,3,2,1,0:T(8,128)(2,1)S(1)} %bitcast.19), channel_id=1, source_target_pairs={{0,8},{8,0},{1,9},{9,1},{2,10},{10,2},{3,11},{11,3},{4,12},{12,4},... | collective-permute-start | bytes 6291464 | tf_op jit(solution)/shard_map/ppermute | solution.py:183
  54.2 4.1 %collective-permute-done.3 = bf16[16,2,8,32,128]{4,3,2,1,0:T(8,128)(2,1)S(1)} collective-permute-done((bf16[16,2,8,32,128]{4,3,2,1,0:T(8,128)(2,1)S(1)}, bf16[16,2,8,32,128]{4,3,2,1,0:T(8,128)(2,1)S(1)}, u32[]{:S(2)}, u32[]{:S(2)}) %collective-permute-start.3) | collective-permute-done | bytes 2097184 | tf_op jit(solution)/shard_map/ppermute | solution.py:183
  58.3 2.1 %fusion = bf16[16,2,8,32,128]{4,3,2,1,0:T(8,128)(2,1)} fusion(bf16[16,2,8,32,128]{4,3,2,1,0:T(8,128)(2,1)S(1)} %bitcast.18, bf16[16,2,8,32,128]{4,3,2,1,0:T(8,128)(2,1)S(1)} %collective-permute-done.3), kind=kLoop, calls=%fused_computation.1 | loop fusion | flops 4194304 | bytes 6291456 | tf_op jit(solution)/shard_map/convert_element_type | solution.py:191
  60.4 5.2 %collective-permute-start.7 = (bf16[32,32,128]{2,1,0:T(8,128)(2,1)S(1)}, bf16[32,32,128]{2,1,0:T(8,128)(2,1)S(1)}, u32[]{:S(2)}, u32[]{:S(2)}) collective-permute-start(bf16[32,32,128]{2,1,0:T(8,128)(2,1)S(1)} %pad_maximum_fusion), channel_id=1, source_target_pairs={{0,32},{32,64},{64,96},{96,128},{128,160},{160,192},{192,224},{224... | collective-permute-start | bytes 786440 | tf_op jit(solution)/shard_map/ppermute | solution.py:212
  65.7 1.9 %collective-permute-start.4 = (bf16[32,32,128]{2,1,0:T(8,128)(2,1)S(1)}, bf16[32,32,128]{2,1,0:T(8,128)(2,1)S(1)}, u32[]{:S(2)}, u32[]{:S(2)}) collective-permute-start(bf16[32,32,128]{2,1,0:T(8,128)(2,1)S(1)} %pad_maximum_fusion), channel_id=1, source_target_pairs={{0,480},{32,0},{64,32},{96,64},{128,96},{160,128},{192,160},{224,1... | collective-permute-start | bytes 786440 | tf_op jit(solution)/shard_map/ppermute | solution.py:212
  67.6 4.2 %collective-permute-done.7 = bf16[32,32,128]{2,1,0:T(8,128)(2,1)S(1)} collective-permute-done((bf16[32,32,128]{2,1,0:T(8,128)(2,1)S(1)}, bf16[32,32,128]{2,1,0:T(8,128)(2,1)S(1)}, u32[]{:S(2)}, u32[]{:S(2)}) %collective-permute-start.7) | collective-permute-done | bytes 262176 | tf_op jit(solution)/shard_map/ppermute | solution.py:212
  71.9 4.0 %collective-permute-start.8 = (bf16[32,32,128]{2,1,0:T(8,128)(2,1)S(1)}, bf16[32,32,128]{2,1,0:T(8,128)(2,1)S(1)}, u32[]{:S(2)}, u32[]{:S(2)}) collective-permute-start(bf16[32,32,128]{2,1,0:T(8,128)(2,1)S(1)} %collective-permute-done.7), channel_id=1, source_target_pairs={{0,32},{32,64},{64,96},{96,128},{128,160},{160,192},{192,224},{224... | collective-permute-start | bytes 786440 | tf_op jit(solution)/shard_map/ppermute | solution.py:212
  75.9 3.1 %collective-permute-start.5 = (bf16[32,32,128]{2,1,0:T(8,128)(2,1)S(1)}, bf16[32,32,128]{2,1,0:T(8,128)(2,1)S(1)}, u32[]{:S(2)}, u32[]{:S(2)}) collective-permute-start(bf16[32,32,128]{2,1,0:T(8,128)(2,1)S(1)} %collective-permute-done.4), channel_id=1, source_target_pairs={{0,480},{32,0},{64,32},{96,64},{128,96},{160,128},{192,160},{224,1... | collective-permute-start | bytes 786440 | tf_op jit(solution)/shard_map/ppermute | solution.py:212
  79.0 3.4 %collective-permute-done.8 = bf16[32,32,128]{2,1,0:T(8,128)(2,1)S(1)} collective-permute-done((bf16[32,32,128]{2,1,0:T(8,128)(2,1)S(1)}, bf16[32,32,128]{2,1,0:T(8,128)(2,1)S(1)}, u32[]{:S(2)}, u32[]{:S(2)}) %collective-permute-start.8) | collective-permute-done | bytes 262176 | tf_op jit(solution)/shard_map/ppermute | solution.py:212
  82.5 3.2 %collective-permute-start.9 = (bf16[32,32,128]{2,1,0:T(8,128)(2,1)S(1)}, bf16[32,32,128]{2,1,0:T(8,128)(2,1)S(1)}, u32[]{:S(2)}, u32[]{:S(2)}) collective-permute-start(bf16[32,32,128]{2,1,0:T(8,128)(2,1)S(1)} %collective-permute-done.8), channel_id=1, source_target_pairs={{0,32},{32,64},{64,96},{96,128},{128,160},{160,192},{192,224},{224... | collective-permute-start | bytes 786440 | tf_op jit(solution)/shard_map/ppermute | solution.py:212
  85.7 1.0 collective-permute-done.5
  86.6 4.4 %collective-permute-start.6 = (bf16[32,32,128]{2,1,0:T(8,128)(2,1)S(1)}, bf16[32,32,128]{2,1,0:T(8,128)(2,1)S(1)}, u32[]{:S(2)}, u32[]{:S(2)}) collective-permute-start(bf16[32,32,128]{2,1,0:T(8,128)(2,1)S(1)} %collective-permute-done.5), channel_id=1, source_target_pairs={{0,480},{32,0},{64,32},{96,64},{128,96},{160,128},{192,160},{224,1... | collective-permute-start | bytes 786440 | tf_op jit(solution)/shard_map/ppermute | solution.py:212
  91.2 4.2 %collective-permute-done.9 = bf16[32,32,128]{2,1,0:T(8,128)(2,1)S(1)} collective-permute-done((bf16[32,32,128]{2,1,0:T(8,128)(2,1)S(1)}, bf16[32,32,128]{2,1,0:T(8,128)(2,1)S(1)}, u32[]{:S(2)}, u32[]{:S(2)}) %collective-permute-start.9) | collective-permute-done | bytes 262176 | tf_op jit(solution)/shard_map/ppermute | solution.py:212
  95.4 1.9 %collective-permute-start.11 = (bf16[16,32,128]{2,1,0:T(8,128)(2,1)S(1)}, bf16[16,32,128]{2,1,0:T(8,128)(2,1)S(1)}, u32[]{:S(2)}, u32[]{:S(2)}) collective-permute-start(bf16[16,32,128]{2,1,0:T(8,128)(2,1)S(1)} %slice.46), channel_id=1, source_target_pairs={{0,32},{32,64},{64,96},{96,128},{128,160},{160,192},{192,224},{224... | collective-permute-start | bytes 393224 | tf_op jit(solution)/shard_map/ppermute | solution.py:212
  97.3 1.7 %collective-permute-done.6 = bf16[32,32,128]{2,1,0:T(8,128)(2,1)S(1)} collective-permute-done((bf16[32,32,128]{2,1,0:T(8,128)(2,1)S(1)}, bf16[32,32,128]{2,1,0:T(8,128)(2,1)S(1)}, u32[]{:S(2)}, u32[]{:S(2)}) %collective-permute-start.6) | collective-permute-done | bytes 262176 | tf_op jit(solution)/shard_map/ppermute | solution.py:212
  99.0 5.6 %collective-permute-start.10 = (bf16[16,32,128]{2,1,0:T(8,128)(2,1)S(1)}, bf16[16,32,128]{2,1,0:T(8,128)(2,1)S(1)}, u32[]{:S(2)}, u32[]{:S(2)}) collective-permute-start(bf16[16,32,128]{2,1,0:T(8,128)(2,1)S(1)} %slice.45), channel_id=1, source_target_pairs={{0,480},{32,0},{64,32},{96,64},{128,96},{160,128},{192,160},{224,1... | collective-permute-start | bytes 393224 | tf_op jit(solution)/shard_map/ppermute | solution.py:212
  104.8 3.4 %collective-permute-done.10 = bf16[16,32,128]{2,1,0:T(8,128)(2,1)S(1)} collective-permute-done((bf16[16,32,128]{2,1,0:T(8,128)(2,1)S(1)}, bf16[16,32,128]{2,1,0:T(8,128)(2,1)S(1)}, u32[]{:S(2)}, u32[]{:S(2)}) %collective-permute-start.10) | collective-permute-done | bytes 131104 | tf_op jit(solution)/shard_map/ppermute | solution.py:212
  108.3 2.1 %collective-permute-start.12 = (bf16[256,32,128]{2,1,0:T(8,128)(2,1)S(1)}, bf16[256,32,128]{2,1,0:T(8,128)(2,1)S(1)}, u32[]{:S(2)}, u32[]{:S(2)}) collective-permute-start(bf16[256,32,128]{2,1,0:T(8,128)(2,1)S(1)} %constant_dynamic-update-slice_fusion.refs_0_), channel_id=1, source_target_pairs={{0,8},{8,0},{1,9},{9,1},{2,10},{10,2},{3,11},{11,3},{4,12},{12,4},... | collective-permute-start | bytes 6291464 | tf_op jit(solution)/shard_map/ppermute | solution.py:183
  110.4 3.9 %collective-permute-done.12.refs_1_ = bf16[256,32,128]{2,1,0:T(8,128)(2,1)S(1)} collective-permute-done((bf16[256,32,128]{2,1,0:T(8,128)(2,1)S(1)}, bf16[256,32,128]{2,1,0:T(8,128)(2,1)S(1)}, u32[]{:S(2)}, u32[]{:S(2)}) %collective-permute-start.12) | collective-permute-done | bytes 2097184 | tf_op jit(solution)/shard_map/ppermute | solution.py:183
  114.4 6.6 %both_passes.1 = (bf16[128,4096]{1,0:T(8,128)(2,1)}, bf16[128,1792]{1,0:T(8,128)(2,1)}, bf16[128,1792]{1,0:T(8,128)(2,1)}) custom-call(s32[448]{0:T(512)S(1)} %reshape.164.cols, s32[448]{0:T(512)S(1)} %get-tuple-element.34.places, bf16[128,1792]{1,0:T(8,128)(2,1)S(1)} %copy-done, bf16[128,1792]{1,0:T(8,128)(2,1)S(1)} %copy-done.1, ...), custom_call_target="tpu_custom_call" | custom-call | flops 1000000 | bytes 65536 | tf_op jit(solution)/shard_map/both_passes/pallas_call | solution.py:162
  121.0 5.7 %all-to-all-start.1 = ((bf16[8,16,4096]{2,1,0:T(8,128)(2,1)}), bf16[8,16,4096]{2,1,0:T(8,128)(2,1)S(1)}, u32[]{:S(2)}, u32[]{:S(2)}) async-start(bf16[8,16,4096]{2,1,0:T(8,128)(2,1)} %bitcast.5), calls=%async_computation.1 | async-start | bytes 2097152 | tf_op jit(solution)/shard_map/all_to_all | solution.py:260
  126.7 12.6 %reduce-scatter.2.cloned.1.call-done = bf16[1,2,8,32,128]{4,3,2,1,0:T(8,128)(2,1)} async-done(((bf16[16,2,8,32,128]{4,3,2,1,0:T(8,128)(2,1)}), bf16[1,2,8,32,128]{4,3,2,1,0:T(8,128)(2,1)}) %reduce-scatter.2.cloned.1.call-update) | async-done | bytes 131088 | tf_op jit(solution)/shard_map/reduce_scatter | solution.py:230
  140.1 3.4 %collective-permute-start.13 = (bf16[8,32,128]{2,1,0:T(8,128)(2,1)S(1)}, bf16[8,32,128]{2,1,0:T(8,128)(2,1)S(1)}, u32[]{:S(2)}, u32[]{:S(2)}) collective-permute-start(bf16[8,32,128]{2,1,0:T(8,128)(2,1)S(1)} %slice_bitcast_fusion), channel_id=1, source_target_pairs={{0,16},{16,0},{1,17},{17,1},{2,18},{18,2},{3,19},{19,3},{4,20},{20... | collective-permute-start | bytes 196616 | tf_op jit(solution)/shard_map/ppermute | solution.py:183
  144.4 3.4 %collective-permute-done.13 = bf16[8,32,128]{2,1,0:T(8,128)(2,1)S(1)} collective-permute-done((bf16[8,32,128]{2,1,0:T(8,128)(2,1)S(1)}, bf16[8,32,128]{2,1,0:T(8,128)(2,1)S(1)}, u32[]{:S(2)}, u32[]{:S(2)}) %collective-permute-start.13) | collective-permute-done | bytes 65568 | tf_op jit(solution)/shard_map/ppermute | solution.py:183
  149.1 1.3 reshape.171
  (49 shorter events, 5.3 us)
Async XLA Ops:
  7.2 8.1 %copy-start.2 = (f32[1,1,8,4096]{3,2,1,0:T(8,128)S(1)}, f32[1,1,8,4096]{3,2,1,0:T(8,128)}, u32[]{:S(2)}) copy-start(f32[1,1,8,4096]{3,2,1,0:T(8,128)} %param.12) | copy-start | bytes 393220
  7.2 31.1 %copy-start.3 = (s32[28,16]{0,1:T(8,128)S(1)}, s32[28,16]{0,1:T(8,128)}, u32[]{:S(2)}) copy-start(s32[28,16]{0,1:T(8,128)} %param.11) | copy-start | bytes 5380
  7.2 31.7 %copy-start.4 = (s32[28,16]{0,1:T(8,128)S(1)}, s32[28,16]{0,1:T(8,128)}, u32[]{:S(2)}) copy-start(s32[28,16]{0,1:T(8,128)} %param.10) | copy-start | bytes 5380
  7.2 40.1 %copy-start.1 = (bf16[128,1792]{1,0:T(8,128)(2,1)S(1)}, bf16[128,1792]{1,0:T(8,128)(2,1)}, u32[]{:S(2)}) copy-start(bf16[128,1792]{1,0:T(8,128)(2,1)} %up.1) | copy-start | bytes 1376260
  7.2 40.1 %copy-start = (bf16[128,1792]{1,0:T(8,128)(2,1)S(1)}, bf16[128,1792]{1,0:T(8,128)(2,1)}, u32[]{:S(2)}) copy-start(bf16[128,1792]{1,0:T(8,128)(2,1)} %gate.1) | copy-start | bytes 1376260
  9.3 38.0 %all-to-all-start = ((bf16[8,16,4096]{2,1,0:T(8,128)(2,1)}), bf16[8,16,4096]{2,1,0:T(8,128)(2,1)S(1)}, u32[]{:S(2)}, u32[]{:S(2)}) async-start(bf16[8,16,4096]{2,1,0:T(8,128)(2,1)} %broadcast_in_dim.2), calls=%async_computation | async-start | bytes 2097152 | tf_op jit(solution)/shard_map/all_to_all | solution.py:206
  15.2 124.1 %reduce-scatter.2.cloned.1.call-start = ((), (), s32[]{:S(2)}) async-start(), calls=%async_computation.3 | async-start | bytes 2228224 | tf_op jit(solution)/shard_map/reduce_scatter | solution.py:230
  15.7 23.4 %collective-permute-start.2 = (bf16[8,32,128]{2,1,0:T(8,128)(2,1)S(1)}, bf16[8,32,128]{2,1,0:T(8,128)(2,1)S(1)}, u32[]{:S(2)}, u32[]{:S(2)}) collective-permute-start(bf16[8,32,128]{2,1,0:T(8,128)(2,1)S(1)} %reshape.168), channel_id=1, source_target_pairs={{0,272},{16,256},{32,304},{48,288},{64,336},{80,320},{96,368},{112... | collective-permute-start | bytes 196616 | tf_op jit(solution)/shard_map/ppermute | solution.py:213
  32.3 15.0 %collective-permute-start.1 = (bf16[8,32,128]{2,1,0:T(8,128)(2,1)S(1)}, bf16[8,32,128]{2,1,0:T(8,128)(2,1)S(1)}, u32[]{:S(2)}, u32[]{:S(2)}) collective-permute-start(bf16[8,32,128]{2,1,0:T(8,128)(2,1)S(1)} %reshape.168), channel_id=1, source_target_pairs={{0,256},{32,288},{64,320},{96,352},{128,384},{160,416},{192,448},{... | collective-permute-start | bytes 196616 | tf_op jit(solution)/shard_map/ppermute | solution.py:212
  34.6 12.7 %collective-permute-start = (bf16[8,32,128]{2,1,0:T(8,128)(2,1)S(1)}, bf16[8,32,128]{2,1,0:T(8,128)(2,1)S(1)}, u32[]{:S(2)}, u32[]{:S(2)}) collective-permute-start(bf16[8,32,128]{2,1,0:T(8,128)(2,1)S(1)} %reshape.168), channel_id=1, source_target_pairs={{0,16},{16,0},{1,17},{17,1},{2,18},{18,2},{3,19},{19,3},{4,20},{20... | collective-permute-start | bytes 196616 | tf_op jit(solution)/shard_map/ppermute | solution.py:183
  52.2 6.1 %collective-permute-start.3 = (bf16[16,2,8,32,128]{4,3,2,1,0:T(8,128)(2,1)S(1)}, bf16[16,2,8,32,128]{4,3,2,1,0:T(8,128)(2,1)S(1)}, u32[]{:S(2)}, u32[]{:S(2)}) collective-permute-start(bf16[16,2,8,32,128]{4,3,2,1,0:T(8,128)(2,1)S(1)} %bitcast.19), channel_id=1, source_target_pairs={{0,8},{8,0},{1,9},{9,1},{2,10},{10,2},{3,11},{11,3},{4,12},{12,4},... | collective-permute-start | bytes 6291464 | tf_op jit(solution)/shard_map/ppermute | solution.py:183
  60.4 11.4 %collective-permute-start.7 = (bf16[32,32,128]{2,1,0:T(8,128)(2,1)S(1)}, bf16[32,32,128]{2,1,0:T(8,128)(2,1)S(1)}, u32[]{:S(2)}, u32[]{:S(2)}) collective-permute-start(bf16[32,32,128]{2,1,0:T(8,128)(2,1)S(1)} %pad_maximum_fusion), channel_id=1, source_target_pairs={{0,32},{32,64},{64,96},{96,128},{128,160},{160,192},{192,224},{224... | collective-permute-start | bytes 786440 | tf_op jit(solution)/shard_map/ppermute | solution.py:212
  65.7 10.2 %collective-permute-start.4 = (bf16[32,32,128]{2,1,0:T(8,128)(2,1)S(1)}, bf16[32,32,128]{2,1,0:T(8,128)(2,1)S(1)}, u32[]{:S(2)}, u32[]{:S(2)}) collective-permute-start(bf16[32,32,128]{2,1,0:T(8,128)(2,1)S(1)} %pad_maximum_fusion), channel_id=1, source_target_pairs={{0,480},{32,0},{64,32},{96,64},{128,96},{160,128},{192,160},{224,1... | collective-permute-start | bytes 786440 | tf_op jit(solution)/shard_map/ppermute | solution.py:212
  71.9 10.6 %collective-permute-start.8 = (bf16[32,32,128]{2,1,0:T(8,128)(2,1)S(1)}, bf16[32,32,128]{2,1,0:T(8,128)(2,1)S(1)}, u32[]{:S(2)}, u32[]{:S(2)}) collective-permute-start(bf16[32,32,128]{2,1,0:T(8,128)(2,1)S(1)} %collective-permute-done.7), channel_id=1, source_target_pairs={{0,32},{32,64},{64,96},{96,128},{128,160},{160,192},{192,224},{224... | collective-permute-start | bytes 786440 | tf_op jit(solution)/shard_map/ppermute | solution.py:212
  75.9 10.7 %collective-permute-start.5 = (bf16[32,32,128]{2,1,0:T(8,128)(2,1)S(1)}, bf16[32,32,128]{2,1,0:T(8,128)(2,1)S(1)}, u32[]{:S(2)}, u32[]{:S(2)}) collective-permute-start(bf16[32,32,128]{2,1,0:T(8,128)(2,1)S(1)} %collective-permute-done.4), channel_id=1, source_target_pairs={{0,480},{32,0},{64,32},{96,64},{128,96},{160,128},{192,160},{224,1... | collective-permute-start | bytes 786440 | tf_op jit(solution)/shard_map/ppermute | solution.py:212
  82.5 12.9 %collective-permute-start.9 = (bf16[32,32,128]{2,1,0:T(8,128)(2,1)S(1)}, bf16[32,32,128]{2,1,0:T(8,128)(2,1)S(1)}, u32[]{:S(2)}, u32[]{:S(2)}) collective-permute-start(bf16[32,32,128]{2,1,0:T(8,128)(2,1)S(1)} %collective-permute-done.8), channel_id=1, source_target_pairs={{0,32},{32,64},{64,96},{96,128},{128,160},{160,192},{192,224},{224... | collective-permute-start | bytes 786440 | tf_op jit(solution)/shard_map/ppermute | solution.py:212
  86.6 12.4 %collective-permute-start.6 = (bf16[32,32,128]{2,1,0:T(8,128)(2,1)S(1)}, bf16[32,32,128]{2,1,0:T(8,128)(2,1)S(1)}, u32[]{:S(2)}, u32[]{:S(2)}) collective-permute-start(bf16[32,32,128]{2,1,0:T(8,128)(2,1)S(1)} %collective-permute-done.5), channel_id=1, source_target_pairs={{0,480},{32,0},{64,32},{96,64},{128,96},{160,128},{192,160},{224,1... | collective-permute-start | bytes 786440 | tf_op jit(solution)/shard_map/ppermute | solution.py:212
  95.4 12.9 %collective-permute-start.11 = (bf16[16,32,128]{2,1,0:T(8,128)(2,1)S(1)}, bf16[16,32,128]{2,1,0:T(8,128)(2,1)S(1)}, u32[]{:S(2)}, u32[]{:S(2)}) collective-permute-start(bf16[16,32,128]{2,1,0:T(8,128)(2,1)S(1)} %slice.46), channel_id=1, source_target_pairs={{0,32},{32,64},{64,96},{96,128},{128,160},{160,192},{192,224},{224... | collective-permute-start | bytes 393224 | tf_op jit(solution)/shard_map/ppermute | solution.py:212
  99.0 9.2 %collective-permute-start.10 = (bf16[16,32,128]{2,1,0:T(8,128)(2,1)S(1)}, bf16[16,32,128]{2,1,0:T(8,128)(2,1)S(1)}, u32[]{:S(2)}, u32[]{:S(2)}) collective-permute-start(bf16[16,32,128]{2,1,0:T(8,128)(2,1)S(1)} %slice.45), channel_id=1, source_target_pairs={{0,480},{32,0},{64,32},{96,64},{128,96},{160,128},{192,160},{224,1... | collective-permute-start | bytes 393224 | tf_op jit(solution)/shard_map/ppermute | solution.py:212
  108.3 6.1 %collective-permute-start.12 = (bf16[256,32,128]{2,1,0:T(8,128)(2,1)S(1)}, bf16[256,32,128]{2,1,0:T(8,128)(2,1)S(1)}, u32[]{:S(2)}, u32[]{:S(2)}) collective-permute-start(bf16[256,32,128]{2,1,0:T(8,128)(2,1)S(1)} %constant_dynamic-update-slice_fusion.refs_0_), channel_id=1, source_target_pairs={{0,8},{8,0},{1,9},{9,1},{2,10},{10,2},{3,11},{11,3},{4,12},{12,4},... | collective-permute-start | bytes 6291464 | tf_op jit(solution)/shard_map/ppermute | solution.py:183
  121.0 22.6 %all-to-all-start.1 = ((bf16[8,16,4096]{2,1,0:T(8,128)(2,1)}), bf16[8,16,4096]{2,1,0:T(8,128)(2,1)S(1)}, u32[]{:S(2)}, u32[]{:S(2)}) async-start(bf16[8,16,4096]{2,1,0:T(8,128)(2,1)} %bitcast.5), calls=%async_computation.1 | async-start | bytes 2097152 | tf_op jit(solution)/shard_map/all_to_all | solution.py:260
  140.1 7.7 %collective-permute-start.13 = (bf16[8,32,128]{2,1,0:T(8,128)(2,1)S(1)}, bf16[8,32,128]{2,1,0:T(8,128)(2,1)S(1)}, u32[]{:S(2)}, u32[]{:S(2)}) collective-permute-start(bf16[8,32,128]{2,1,0:T(8,128)(2,1)S(1)} %slice_bitcast_fusion), channel_id=1, source_target_pairs={{0,16},{16,0},{1,17},{17,1},{2,18},{18,2},{3,19},{19,3},{4,20},{20... | collective-permute-start | bytes 196616 | tf_op jit(solution)/shard_map/ppermute | solution.py:183
Sparse Core Ops, SparseCore 0:
  67.8 71.4 reduce-scatter.1

commit v3 on v2

--- a/solution.py
+++ b/solution.py
@@ -206,7 +206,6 @@
     full_grad = lax.all_to_all(
         copies, ("x_lo", "y"), split_axis=0, concat_axis=0, tiled=True
     ).reshape(row_count, width)
-    stored = after(stored, copies)
     away = depth // 2
     across = [((z * 2 + x), ((z + away) % depth) * 2 + 1 - x) for z in range(depth) for x in range(2)]
     shift = lambda x, by: lax.ppermute(x, Z, [(z, (z + by) % depth) for z in range(depth)])

time: 158 us -> 158 us (level)
  no operation moved by 1% of the time
where the time goes in v3:
time: 158 us; the launch traced here: 157 us
  starting transfers between devices  71 us (45%)
  waiting for transfers between devices  50.2 us (32%)
  between operations  14.4 us (9%)
  Pallas kernels  10.9 us (7%)
  local copies, waits for them, and re-layouts  6.6 us (4%)
  other arithmetic  4.22 us (3%)
    ppermute x9, starting transfers between devices, on_device(): lax.ppermute(x, Z, [(z, (z + by) % depth) for z in range(depth)])  31.7 us
    ppermute x9, waiting for transfers between devices, on_device(): lax.ppermute(x, Z, [(z, (z + by) % depth) for z in range(depth)])  26.1 us
    ppermute x1, starting transfers between devices, on_device(): lax.ppermute(stored, Z + ('x_hi',), across)  16.6 us
    reduce_scatter x1, waiting for transfers between devices, on_device(): line = lax.psum_scatter(chip, Z, scatter_dimension=0, tiled=False)  12.6 us
    ppermute x4, waiting for transfers between devices, swap(): return lax.ppermute(x, axis, [(0, 1), (1, 0)])  11.4 us
    ppermute x4, starting transfers between devices, swap(): return lax.ppermute(x, axis, [(0, 1), (1, 0)])  11.2 us
    pallas_call x1, Pallas kernels, both_passes(): pl.pallas_call(passes_kernel, out_shape=(jax.ShapeDtypeStruct((rows, col_...  6.63 us
    all_to_all x1, starting transfers between devices, on_device(): lax.all_to_all(copies, ('x_lo', 'y'), split_axis=0, concat_axis=0, tiled=...  5.93 us
  transfers between devices with their start and end apart: 17, of which 11 were waited for; matrix products, arithmetic and copies ran while one was open for 2% of the time, Pallas kernels for 4%

profile of v3, /device:TPU:6, one launch (start us, length us, event | category | flops | bytes accessed | tf_op | source)
XLA Modules:
  0.0 157.3 jit_solution(782940151168235150)
XLA Ops:
  7.2 2.1 %broadcast_in_dim.2 = bf16[8,16,4096]{2,1,0:T(8,128)(2,1)} broadcast(bf16[16,4096]{1,0:T(8,128)(2,1)} %param.9), dimensions={1,2} | broadcast | bytes 1179648 | tf_op jit(solution)/shard_map/broadcast_in_dim | solution.py:205
  9.3 5.9 %all-to-all-start = ((bf16[8,16,4096]{2,1,0:T(8,128)(2,1)}), bf16[8,16,4096]{2,1,0:T(8,128)(2,1)S(1)}, u32[]{:S(2)}, u32[]{:S(2)}) async-start(bf16[8,16,4096]{2,1,0:T(8,128)(2,1)} %broadcast_in_dim.2), calls=%async_computation | async-start | bytes 2097152 | tf_op jit(solution)/shard_map/all_to_all | solution.py:206
  15.7 16.6 %collective-permute-start.2 = (bf16[8,32,128]{2,1,0:T(8,128)(2,1)S(1)}, bf16[8,32,128]{2,1,0:T(8,128)(2,1)S(1)}, u32[]{:S(2)}, u32[]{:S(2)}) collective-permute-start(bf16[8,32,128]{2,1,0:T(8,128)(2,1)S(1)} %reshape.168), channel_id=1, source_target_pairs={{0,272},{16,256},{32,304},{48,288},{64,336},{80,320},{96,368},{112... | collective-permute-start | bytes 196616 | tf_op jit(solution)/shard_map/ppermute | solution.py:212
  32.3 2.3 %collective-permute-start.1 = (bf16[8,32,128]{2,1,0:T(8,128)(2,1)S(1)}, bf16[8,32,128]{2,1,0:T(8,128)(2,1)S(1)}, u32[]{:S(2)}, u32[]{:S(2)}) collective-permute-start(bf16[8,32,128]{2,1,0:T(8,128)(2,1)S(1)} %reshape.168), channel_id=1, source_target_pairs={{0,256},{32,288},{64,320},{96,352},{128,384},{160,416},{192,448},{... | collective-permute-start | bytes 196616 | tf_op jit(solution)/shard_map/ppermute | solution.py:211
  34.6 3.7 %collective-permute-start = (bf16[8,32,128]{2,1,0:T(8,128)(2,1)S(1)}, bf16[8,32,128]{2,1,0:T(8,128)(2,1)S(1)}, u32[]{:S(2)}, u32[]{:S(2)}) collective-permute-start(bf16[8,32,128]{2,1,0:T(8,128)(2,1)S(1)} %reshape.168), channel_id=1, source_target_pairs={{0,16},{16,0},{1,17},{17,1},{2,18},{18,2},{3,19},{19,3},{4,20},{20... | collective-permute-start | bytes 196616 | tf_op jit(solution)/shard_map/ppermute | solution.py:183
  39.1 8.2 %collective-permute-done.1 = bf16[8,32,128]{2,1,0:T(8,128)(2,1)S(1)} collective-permute-done((bf16[8,32,128]{2,1,0:T(8,128)(2,1)S(1)}, bf16[8,32,128]{2,1,0:T(8,128)(2,1)S(1)}, u32[]{:S(2)}, u32[]{:S(2)}) %collective-permute-start.1) | collective-permute-done | bytes 65568 | tf_op jit(solution)/shard_map/ppermute | solution.py:211
  47.3 4.2 %block_grads.1 = (bf16[512,32,128]{2,1,0:T(8,128)(2,1)S(1)}, bf16[64,32,256]{2,1,0:T(8,128)(2,1)S(1)}) custom-call(s32[448]{0:T(512)S(1)} %reshape.164.cols, s32[448]{0:T(512)S(1)} %get-tuple-element.31.places, bf16[128,1792]{1,0:T(8,128)(2,1)S(1)} %copy-done, bf16[128,1792]{1,0:T(8,128)(2,1)S(1)} %copy-done.1, bf16[128,4096]{1,0:T(8,128)(2,1)S(1)} %bitcast.17), custom_call_target="tpu_custom_call" | custom-call | flops 8999999488 | bytes 7340032 | tf_op jit(solution)/shard_map/block_grads/pallas_call | solution.py:139
  52.2 1.9 %collective-permute-start.3 = (bf16[16,2,8,32,128]{4,3,2,1,0:T(8,128)(2,1)S(1)}, bf16[16,2,8,32,128]{4,3,2,1,0:T(8,128)(2,1)S(1)}, u32[]{:S(2)}, u32[]{:S(2)}) collective-permute-start(bf16[16,2,8,32,128]{4,3,2,1,0:T(8,128)(2,1)S(1)} %bitcast.19), channel_id=1, source_target_pairs={{0,8},{8,0},{1,9},{9,1},{2,10},{10,2},{3,11},{11,3},{4,12},{12,4},... | collective-permute-start | bytes 6291464 | tf_op jit(solution)/shard_map/ppermute | solution.py:183
  54.2 4.1 %collective-permute-done.3 = bf16[16,2,8,32,128]{4,3,2,1,0:T(8,128)(2,1)S(1)} collective-permute-done((bf16[16,2,8,32,128]{4,3,2,1,0:T(8,128)(2,1)S(1)}, bf16[16,2,8,32,128]{4,3,2,1,0:T(8,128)(2,1)S(1)}, u32[]{:S(2)}, u32[]{:S(2)}) %collective-permute-start.3) | collective-permute-done | bytes 2097184 | tf_op jit(solution)/shard_map/ppermute | solution.py:183
  58.3 2.1 %fusion = bf16[16,2,8,32,128]{4,3,2,1,0:T(8,128)(2,1)} fusion(bf16[16,2,8,32,128]{4,3,2,1,0:T(8,128)(2,1)S(1)} %bitcast.18, bf16[16,2,8,32,128]{4,3,2,1,0:T(8,128)(2,1)S(1)} %collective-permute-done.3), kind=kLoop, calls=%fused_computation.1 | loop fusion | flops 4194304 | bytes 6291456 | tf_op jit(solution)/shard_map/convert_element_type | solution.py:191
  60.4 5.2 %collective-permute-start.7 = (bf16[32,32,128]{2,1,0:T(8,128)(2,1)S(1)}, bf16[32,32,128]{2,1,0:T(8,128)(2,1)S(1)}, u32[]{:S(2)}, u32[]{:S(2)}) collective-permute-start(bf16[32,32,128]{2,1,0:T(8,128)(2,1)S(1)} %pad_maximum_fusion), channel_id=1, source_target_pairs={{0,32},{32,64},{64,96},{96,128},{128,160},{160,192},{192,224},{224... | collective-permute-start | bytes 786440 | tf_op jit(solution)/shard_map/ppermute | solution.py:211
  65.7 1.9 %collective-permute-start.4 = (bf16[32,32,128]{2,1,0:T(8,128)(2,1)S(1)}, bf16[32,32,128]{2,1,0:T(8,128)(2,1)S(1)}, u32[]{:S(2)}, u32[]{:S(2)}) collective-permute-start(bf16[32,32,128]{2,1,0:T(8,128)(2,1)S(1)} %pad_maximum_fusion), channel_id=1, source_target_pairs={{0,480},{32,0},{64,32},{96,64},{128,96},{160,128},{192,160},{224,1... | collective-permute-start | bytes 786440 | tf_op jit(solution)/shard_map/ppermute | solution.py:211
  67.6 4.2 %collective-permute-done.7 = bf16[32,32,128]{2,1,0:T(8,128)(2,1)S(1)} collective-permute-done((bf16[32,32,128]{2,1,0:T(8,128)(2,1)S(1)}, bf16[32,32,128]{2,1,0:T(8,128)(2,1)S(1)}, u32[]{:S(2)}, u32[]{:S(2)}) %collective-permute-start.7) | collective-permute-done | bytes 262176 | tf_op jit(solution)/shard_map/ppermute | solution.py:211
  71.9 4.0 %collective-permute-start.8 = (bf16[32,32,128]{2,1,0:T(8,128)(2,1)S(1)}, bf16[32,32,128]{2,1,0:T(8,128)(2,1)S(1)}, u32[]{:S(2)}, u32[]{:S(2)}) collective-permute-start(bf16[32,32,128]{2,1,0:T(8,128)(2,1)S(1)} %collective-permute-done.7), channel_id=1, source_target_pairs={{0,32},{32,64},{64,96},{96,128},{128,160},{160,192},{192,224},{224... | collective-permute-start | bytes 786440 | tf_op jit(solution)/shard_map/ppermute | solution.py:211
  75.9 3.1 %collective-permute-start.5 = (bf16[32,32,128]{2,1,0:T(8,128)(2,1)S(1)}, bf16[32,32,128]{2,1,0:T(8,128)(2,1)S(1)}, u32[]{:S(2)}, u32[]{:S(2)}) collective-permute-start(bf16[32,32,128]{2,1,0:T(8,128)(2,1)S(1)} %collective-permute-done.4), channel_id=1, source_target_pairs={{0,480},{32,0},{64,32},{96,64},{128,96},{160,128},{192,160},{224,1... | collective-permute-start | bytes 786440 | tf_op jit(solution)/shard_map/ppermute | solution.py:211
  79.0 3.4 %collective-permute-done.8 = bf16[32,32,128]{2,1,0:T(8,128)(2,1)S(1)} collective-permute-done((bf16[32,32,128]{2,1,0:T(8,128)(2,1)S(1)}, bf16[32,32,128]{2,1,0:T(8,128)(2,1)S(1)}, u32[]{:S(2)}, u32[]{:S(2)}) %collective-permute-start.8) | collective-permute-done | bytes 262176 | tf_op jit(solution)/shard_map/ppermute | solution.py:211
  82.5 3.2 %collective-permute-start.9 = (bf16[32,32,128]{2,1,0:T(8,128)(2,1)S(1)}, bf16[32,32,128]{2,1,0:T(8,128)(2,1)S(1)}, u32[]{:S(2)}, u32[]{:S(2)}) collective-permute-start(bf16[32,32,128]{2,1,0:T(8,128)(2,1)S(1)} %collective-permute-done.8), channel_id=1, source_target_pairs={{0,32},{32,64},{64,96},{96,128},{128,160},{160,192},{192,224},{224... | collective-permute-start | bytes 786440 | tf_op jit(solution)/shard_map/ppermute | solution.py:211
  85.7 1.0 collective-permute-done.5
  86.6 4.4 %collective-permute-start.6 = (bf16[32,32,128]{2,1,0:T(8,128)(2,1)S(1)}, bf16[32,32,128]{2,1,0:T(8,128)(2,1)S(1)}, u32[]{:S(2)}, u32[]{:S(2)}) collective-permute-start(bf16[32,32,128]{2,1,0:T(8,128)(2,1)S(1)} %collective-permute-done.5), channel_id=1, source_target_pairs={{0,480},{32,0},{64,32},{96,64},{128,96},{160,128},{192,160},{224,1... | collective-permute-start | bytes 786440 | tf_op jit(solution)/shard_map/ppermute | solution.py:211
  91.2 4.2 %collective-permute-done.9 = bf16[32,32,128]{2,1,0:T(8,128)(2,1)S(1)} collective-permute-done((bf16[32,32,128]{2,1,0:T(8,128)(2,1)S(1)}, bf16[32,32,128]{2,1,0:T(8,128)(2,1)S(1)}, u32[]{:S(2)}, u32[]{:S(2)}) %collective-permute-start.9) | collective-permute-done | bytes 262176 | tf_op jit(solution)/shard_map/ppermute | solution.py:211
  95.4 1.9 %collective-permute-start.11 = (bf16[16,32,128]{2,1,0:T(8,128)(2,1)S(1)}, bf16[16,32,128]{2,1,0:T(8,128)(2,1)S(1)}, u32[]{:S(2)}, u32[]{:S(2)}) collective-permute-start(bf16[16,32,128]{2,1,0:T(8,128)(2,1)S(1)} %slice.46), channel_id=1, source_target_pairs={{0,32},{32,64},{64,96},{96,128},{128,160},{160,192},{192,224},{224... | collective-permute-start | bytes 393224 | tf_op jit(solution)/shard_map/ppermute | solution.py:211
  97.3 1.7 %collective-permute-done.6 = bf16[32,32,128]{2,1,0:T(8,128)(2,1)S(1)} collective-permute-done((bf16[32,32,128]{2,1,0:T(8,128)(2,1)S(1)}, bf16[32,32,128]{2,1,0:T(8,128)(2,1)S(1)}, u32[]{:S(2)}, u32[]{:S(2)}) %collective-permute-start.6) | collective-permute-done | bytes 262176 | tf_op jit(solution)/shard_map/ppermute | solution.py:211
  99.0 5.6 %collective-permute-start.10 = (bf16[16,32,128]{2,1,0:T(8,128)(2,1)S(1)}, bf16[16,32,128]{2,1,0:T(8,128)(2,1)S(1)}, u32[]{:S(2)}, u32[]{:S(2)}) collective-permute-start(bf16[16,32,128]{2,1,0:T(8,128)(2,1)S(1)} %slice.45), channel_id=1, source_target_pairs={{0,480},{32,0},{64,32},{96,64},{128,96},{160,128},{192,160},{224,1... | collective-permute-start | bytes 393224 | tf_op jit(solution)/shard_map/ppermute | solution.py:211
  104.8 3.4 %collective-permute-done.10 = bf16[16,32,128]{2,1,0:T(8,128)(2,1)S(1)} collective-permute-done((bf16[16,32,128]{2,1,0:T(8,128)(2,1)S(1)}, bf16[16,32,128]{2,1,0:T(8,128)(2,1)S(1)}, u32[]{:S(2)}, u32[]{:S(2)}) %collective-permute-start.10) | collective-permute-done | bytes 131104 | tf_op jit(solution)/shard_map/ppermute | solution.py:211
  108.3 2.1 %collective-permute-start.12 = (bf16[256,32,128]{2,1,0:T(8,128)(2,1)S(1)}, bf16[256,32,128]{2,1,0:T(8,128)(2,1)S(1)}, u32[]{:S(2)}, u32[]{:S(2)}) collective-permute-start(bf16[256,32,128]{2,1,0:T(8,128)(2,1)S(1)} %constant_dynamic-update-slice_fusion.refs_0_), channel_id=1, source_target_pairs={{0,8},{8,0},{1,9},{9,1},{2,10},{10,2},{3,11},{11,3},{4,12},{12,4},... | collective-permute-start | bytes 6291464 | tf_op jit(solution)/shard_map/ppermute | solution.py:183
  110.4 3.9 %collective-permute-done.12.refs_1_ = bf16[256,32,128]{2,1,0:T(8,128)(2,1)S(1)} collective-permute-done((bf16[256,32,128]{2,1,0:T(8,128)(2,1)S(1)}, bf16[256,32,128]{2,1,0:T(8,128)(2,1)S(1)}, u32[]{:S(2)}, u32[]{:S(2)}) %collective-permute-start.12) | collective-permute-done | bytes 2097184 | tf_op jit(solution)/shard_map/ppermute | solution.py:183
  114.4 6.6 %both_passes.1 = (bf16[128,4096]{1,0:T(8,128)(2,1)}, bf16[128,1792]{1,0:T(8,128)(2,1)}, bf16[128,1792]{1,0:T(8,128)(2,1)}) custom-call(s32[448]{0:T(512)S(1)} %reshape.164.cols, s32[448]{0:T(512)S(1)} %get-tuple-element.32.places, bf16[128,1792]{1,0:T(8,128)(2,1)S(1)} %copy-done, bf16[128,1792]{1,0:T(8,128)(2,1)S(1)} %copy-done.1, ...), custom_call_target="tpu_custom_call" | custom-call | flops 1000000 | bytes 65536 | tf_op jit(solution)/shard_map/both_passes/pallas_call | solution.py:162
  121.0 5.7 %all-to-all-start.1 = ((bf16[8,16,4096]{2,1,0:T(8,128)(2,1)}), bf16[8,16,4096]{2,1,0:T(8,128)(2,1)S(1)}, u32[]{:S(2)}, u32[]{:S(2)}) async-start(bf16[8,16,4096]{2,1,0:T(8,128)(2,1)} %bitcast.5), calls=%async_computation.1 | async-start | bytes 2097152 | tf_op jit(solution)/shard_map/all_to_all | solution.py:259
  126.7 12.6 %reduce-scatter.2.cloned.1.call-done = bf16[1,2,8,32,128]{4,3,2,1,0:T(8,128)(2,1)} async-done(((bf16[16,2,8,32,128]{4,3,2,1,0:T(8,128)(2,1)}), bf16[1,2,8,32,128]{4,3,2,1,0:T(8,128)(2,1)}) %reduce-scatter.2.cloned.1.call-update) | async-done | bytes 131088 | tf_op jit(solution)/shard_map/reduce_scatter | solution.py:229
  140.1 3.5 %collective-permute-start.13 = (bf16[8,32,128]{2,1,0:T(8,128)(2,1)S(1)}, bf16[8,32,128]{2,1,0:T(8,128)(2,1)S(1)}, u32[]{:S(2)}, u32[]{:S(2)}) collective-permute-start(bf16[8,32,128]{2,1,0:T(8,128)(2,1)S(1)} %slice_bitcast_fusion), channel_id=1, source_target_pairs={{0,16},{16,0},{1,17},{17,1},{2,18},{18,2},{3,19},{19,3},{4,20},{20... | collective-permute-start | bytes 196616 | tf_op jit(solution)/shard_map/ppermute | solution.py:183
  144.4 3.3 %collective-permute-done.13 = bf16[8,32,128]{2,1,0:T(8,128)(2,1)S(1)} collective-permute-done((bf16[8,32,128]{2,1,0:T(8,128)(2,1)S(1)}, bf16[8,32,128]{2,1,0:T(8,128)(2,1)S(1)}, u32[]{:S(2)}, u32[]{:S(2)}) %collective-permute-start.13) | collective-permute-done | bytes 65568 | tf_op jit(solution)/shard_map/ppermute | solution.py:183
  149.1 1.3 reshape.171
  (49 shorter events, 5.3 us)
Async XLA Ops:
  7.2 8.1 %copy-start.2 = (f32[1,1,8,4096]{3,2,1,0:T(8,128)S(1)}, f32[1,1,8,4096]{3,2,1,0:T(8,128)}, u32[]{:S(2)}) copy-start(f32[1,1,8,4096]{3,2,1,0:T(8,128)} %param.12) | copy-start | bytes 393220
  7.2 31.1 %copy-start.3 = (s32[28,16]{0,1:T(8,128)S(1)}, s32[28,16]{0,1:T(8,128)}, u32[]{:S(2)}) copy-start(s32[28,16]{0,1:T(8,128)} %param.11) | copy-start | bytes 5380
  7.2 31.7 %copy-start.4 = (s32[28,16]{0,1:T(8,128)S(1)}, s32[28,16]{0,1:T(8,128)}, u32[]{:S(2)}) copy-start(s32[28,16]{0,1:T(8,128)} %param.10) | copy-start | bytes 5380
  7.2 40.1 %copy-start.1 = (bf16[128,1792]{1,0:T(8,128)(2,1)S(1)}, bf16[128,1792]{1,0:T(8,128)(2,1)}, u32[]{:S(2)}) copy-start(bf16[128,1792]{1,0:T(8,128)(2,1)} %up.1) | copy-start | bytes 1376260
  7.2 40.1 %copy-start = (bf16[128,1792]{1,0:T(8,128)(2,1)S(1)}, bf16[128,1792]{1,0:T(8,128)(2,1)}, u32[]{:S(2)}) copy-start(bf16[128,1792]{1,0:T(8,128)(2,1)} %gate.1) | copy-start | bytes 1376260
  9.3 38.0 %all-to-all-start = ((bf16[8,16,4096]{2,1,0:T(8,128)(2,1)}), bf16[8,16,4096]{2,1,0:T(8,128)(2,1)S(1)}, u32[]{:S(2)}, u32[]{:S(2)}) async-start(bf16[8,16,4096]{2,1,0:T(8,128)(2,1)} %broadcast_in_dim.2), calls=%async_computation | async-start | bytes 2097152 | tf_op jit(solution)/shard_map/all_to_all | solution.py:206
  15.2 124.1 %reduce-scatter.2.cloned.1.call-start = ((), (), s32[]{:S(2)}) async-start(), calls=%async_computation.3 | async-start | bytes 2228224 | tf_op jit(solution)/shard_map/reduce_scatter | solution.py:229
  15.7 23.4 %collective-permute-start.2 = (bf16[8,32,128]{2,1,0:T(8,128)(2,1)S(1)}, bf16[8,32,128]{2,1,0:T(8,128)(2,1)S(1)}, u32[]{:S(2)}, u32[]{:S(2)}) collective-permute-start(bf16[8,32,128]{2,1,0:T(8,128)(2,1)S(1)} %reshape.168), channel_id=1, source_target_pairs={{0,272},{16,256},{32,304},{48,288},{64,336},{80,320},{96,368},{112... | collective-permute-start | bytes 196616 | tf_op jit(solution)/shard_map/ppermute | solution.py:212
  32.3 15.0 %collective-permute-start.1 = (bf16[8,32,128]{2,1,0:T(8,128)(2,1)S(1)}, bf16[8,32,128]{2,1,0:T(8,128)(2,1)S(1)}, u32[]{:S(2)}, u32[]{:S(2)}) collective-permute-start(bf16[8,32,128]{2,1,0:T(8,128)(2,1)S(1)} %reshape.168), channel_id=1, source_target_pairs={{0,256},{32,288},{64,320},{96,352},{128,384},{160,416},{192,448},{... | collective-permute-start | bytes 196616 | tf_op jit(solution)/shard_map/ppermute | solution.py:211
  34.6 12.7 %collective-permute-start = (bf16[8,32,128]{2,1,0:T(8,128)(2,1)S(1)}, bf16[8,32,128]{2,1,0:T(8,128)(2,1)S(1)}, u32[]{:S(2)}, u32[]{:S(2)}) collective-permute-start(bf16[8,32,128]{2,1,0:T(8,128)(2,1)S(1)} %reshape.168), channel_id=1, source_target_pairs={{0,16},{16,0},{1,17},{17,1},{2,18},{18,2},{3,19},{19,3},{4,20},{20... | collective-permute-start | bytes 196616 | tf_op jit(solution)/shard_map/ppermute | solution.py:183
  52.2 6.1 %collective-permute-start.3 = (bf16[16,2,8,32,128]{4,3,2,1,0:T(8,128)(2,1)S(1)}, bf16[16,2,8,32,128]{4,3,2,1,0:T(8,128)(2,1)S(1)}, u32[]{:S(2)}, u32[]{:S(2)}) collective-permute-start(bf16[16,2,8,32,128]{4,3,2,1,0:T(8,128)(2,1)S(1)} %bitcast.19), channel_id=1, source_target_pairs={{0,8},{8,0},{1,9},{9,1},{2,10},{10,2},{3,11},{11,3},{4,12},{12,4},... | collective-permute-start | bytes 6291464 | tf_op jit(solution)/shard_map/ppermute | solution.py:183
  60.4 11.4 %collective-permute-start.7 = (bf16[32,32,128]{2,1,0:T(8,128)(2,1)S(1)}, bf16[32,32,128]{2,1,0:T(8,128)(2,1)S(1)}, u32[]{:S(2)}, u32[]{:S(2)}) collective-permute-start(bf16[32,32,128]{2,1,0:T(8,128)(2,1)S(1)} %pad_maximum_fusion), channel_id=1, source_target_pairs={{0,32},{32,64},{64,96},{96,128},{128,160},{160,192},{192,224},{224... | collective-permute-start | bytes 786440 | tf_op jit(solution)/shard_map/ppermute | solution.py:211
  65.7 10.2 %collective-permute-start.4 = (bf16[32,32,128]{2,1,0:T(8,128)(2,1)S(1)}, bf16[32,32,128]{2,1,0:T(8,128)(2,1)S(1)}, u32[]{:S(2)}, u32[]{:S(2)}) collective-permute-start(bf16[32,32,128]{2,1,0:T(8,128)(2,1)S(1)} %pad_maximum_fusion), channel_id=1, source_target_pairs={{0,480},{32,0},{64,32},{96,64},{128,96},{160,128},{192,160},{224,1... | collective-permute-start | bytes 786440 | tf_op jit(solution)/shard_map/ppermute | solution.py:211
  71.9 10.6 %collective-permute-start.8 = (bf16[32,32,128]{2,1,0:T(8,128)(2,1)S(1)}, bf16[32,32,128]{2,1,0:T(8,128)(2,1)S(1)}, u32[]{:S(2)}, u32[]{:S(2)}) collective-permute-start(bf16[32,32,128]{2,1,0:T(8,128)(2,1)S(1)} %collective-permute-done.7), channel_id=1, source_target_pairs={{0,32},{32,64},{64,96},{96,128},{128,160},{160,192},{192,224},{224... | collective-permute-start | bytes 786440 | tf_op jit(solution)/shard_map/ppermute | solution.py:211
  75.9 10.7 %collective-permute-start.5 = (bf16[32,32,128]{2,1,0:T(8,128)(2,1)S(1)}, bf16[32,32,128]{2,1,0:T(8,128)(2,1)S(1)}, u32[]{:S(2)}, u32[]{:S(2)}) collective-permute-start(bf16[32,32,128]{2,1,0:T(8,128)(2,1)S(1)} %collective-permute-done.4), channel_id=1, source_target_pairs={{0,480},{32,0},{64,32},{96,64},{128,96},{160,128},{192,160},{224,1... | collective-permute-start | bytes 786440 | tf_op jit(solution)/shard_map/ppermute | solution.py:211
  82.5 12.9 %collective-permute-start.9 = (bf16[32,32,128]{2,1,0:T(8,128)(2,1)S(1)}, bf16[32,32,128]{2,1,0:T(8,128)(2,1)S(1)}, u32[]{:S(2)}, u32[]{:S(2)}) collective-permute-start(bf16[32,32,128]{2,1,0:T(8,128)(2,1)S(1)} %collective-permute-done.8), channel_id=1, source_target_pairs={{0,32},{32,64},{64,96},{96,128},{128,160},{160,192},{192,224},{224... | collective-permute-start | bytes 786440 | tf_op jit(solution)/shard_map/ppermute | solution.py:211
  86.6 12.4 %collective-permute-start.6 = (bf16[32,32,128]{2,1,0:T(8,128)(2,1)S(1)}, bf16[32,32,128]{2,1,0:T(8,128)(2,1)S(1)}, u32[]{:S(2)}, u32[]{:S(2)}) collective-permute-start(bf16[32,32,128]{2,1,0:T(8,128)(2,1)S(1)} %collective-permute-done.5), channel_id=1, source_target_pairs={{0,480},{32,0},{64,32},{96,64},{128,96},{160,128},{192,160},{224,1... | collective-permute-start | bytes 786440 | tf_op jit(solution)/shard_map/ppermute | solution.py:211
  95.4 12.9 %collective-permute-start.11 = (bf16[16,32,128]{2,1,0:T(8,128)(2,1)S(1)}, bf16[16,32,128]{2,1,0:T(8,128)(2,1)S(1)}, u32[]{:S(2)}, u32[]{:S(2)}) collective-permute-start(bf16[16,32,128]{2,1,0:T(8,128)(2,1)S(1)} %slice.46), channel_id=1, source_target_pairs={{0,32},{32,64},{64,96},{96,128},{128,160},{160,192},{192,224},{224... | collective-permute-start | bytes 393224 | tf_op jit(solution)/shard_map/ppermute | solution.py:211
  99.0 9.2 %collective-permute-start.10 = (bf16[16,32,128]{2,1,0:T(8,128)(2,1)S(1)}, bf16[16,32,128]{2,1,0:T(8,128)(2,1)S(1)}, u32[]{:S(2)}, u32[]{:S(2)}) collective-permute-start(bf16[16,32,128]{2,1,0:T(8,128)(2,1)S(1)} %slice.45), channel_id=1, source_target_pairs={{0,480},{32,0},{64,32},{96,64},{128,96},{160,128},{192,160},{224,1... | collective-permute-start | bytes 393224 | tf_op jit(solution)/shard_map/ppermute | solution.py:211
  108.3 6.1 %collective-permute-start.12 = (bf16[256,32,128]{2,1,0:T(8,128)(2,1)S(1)}, bf16[256,32,128]{2,1,0:T(8,128)(2,1)S(1)}, u32[]{:S(2)}, u32[]{:S(2)}) collective-permute-start(bf16[256,32,128]{2,1,0:T(8,128)(2,1)S(1)} %constant_dynamic-update-slice_fusion.refs_0_), channel_id=1, source_target_pairs={{0,8},{8,0},{1,9},{9,1},{2,10},{10,2},{3,11},{11,3},{4,12},{12,4},... | collective-permute-start | bytes 6291464 | tf_op jit(solution)/shard_map/ppermute | solution.py:183
  121.0 22.6 %all-to-all-start.1 = ((bf16[8,16,4096]{2,1,0:T(8,128)(2,1)}), bf16[8,16,4096]{2,1,0:T(8,128)(2,1)S(1)}, u32[]{:S(2)}, u32[]{:S(2)}) async-start(bf16[8,16,4096]{2,1,0:T(8,128)(2,1)} %bitcast.5), calls=%async_computation.1 | async-start | bytes 2097152 | tf_op jit(solution)/shard_map/all_to_all | solution.py:259
  140.1 7.7 %collective-permute-start.13 = (bf16[8,32,128]{2,1,0:T(8,128)(2,1)S(1)}, bf16[8,32,128]{2,1,0:T(8,128)(2,1)S(1)}, u32[]{:S(2)}, u32[]{:S(2)}) collective-permute-start(bf16[8,32,128]{2,1,0:T(8,128)(2,1)S(1)} %slice_bitcast_fusion), channel_id=1, source_target_pairs={{0,16},{16,0},{1,17},{17,1},{2,18},{18,2},{3,19},{19,3},{4,20},{20... | collective-permute-start | bytes 196616 | tf_op jit(solution)/shard_map/ppermute | solution.py:183
Sparse Core Ops, SparseCore 0:
  67.8 71.4 reduce-scatter.1
